TPU v7x, 256 devices: a whole 4x4x8 slice. The times are simulated.
256 devices in a mesh: src: 8 (over z), tgt: 32 (over y, x, core).
Axes of the slice: x: 4, y: 4, z: 8, core: 2. Of those that a mesh axis runs over, the one named last changes fastest.
Arguments:
- src_cells: bfloat16 [64, 131072], P(None, 'src'), may hold values from -6 to 6
- tgt_cells: bfloat16 [64, 131072], P(None, 'tgt'), may hold values from -2 to 2
- src_logmass: float32 [131072], P('src'), may hold values from -1 to 1
- tgt_logmass: float32 [131072], P('tgt'), may hold values from -1 to 1
- init_potential: float32 [131072], P('tgt'), may hold values from -1 to 60
- pattern: int32 [256, 256], P('src', 'tgt'), may hold values from 0 to 1, as said below
Outputs:
- src_potential: float32 [131072], P('src')
- tgt_potential: float32 [131072], P('tgt')
Inputs may be any that keep to these rules, and one draw needn't show every extreme that they name: pattern[i, j] = 1 marks source block i (cells i * 512 to (i + 1) * 512 - 1) and target block j as an active pair, 0 an inactive one; pattern[i, i mod 256] = 1 for every source block i.
All inputs are finite; a program needn't handle non-finite values.
Results may differ from a plain program's by a relative error of at most 0.0005.
Values sent between devices are 32-bit elements; how exact they have to be, the bound alone decides.
No kernel may reach another device: no remote copies, remote signals or barrier semaphores. Data moves between devices by JAX's collectives and lax.ppermute only.
A program may use at most 64 MiB of HBM per device.

v0:
```python
import jax
import jax.numpy as jnp
from jax import lax
from jax.sharding import PartitionSpec as P

BLOCK = 512
SWEEPS = 2


entropy = 0.5
lowest = -1e30


def block_lse(row_cells, col_cells, row_sq, col_sq, col_pot, pair_mask):
    group_size = 8
    feature_dim = row_cells.shape[0]
    row_span, col_span = pair_mask.shape
    block_width = row_sq.shape[1]
    row_blocks = row_cells.reshape(feature_dim, row_span, block_width)
    col_blocks = col_cells.reshape(feature_dim, col_span, block_width)
    flat_mask = pair_mask.reshape(-1)
    slot_count = flat_mask.shape[0]
    slot_ids = jnp.arange(slot_count, dtype=jnp.int32)
    active_order = jnp.argsort((1 - flat_mask) * slot_count + slot_ids)
    active_order = jnp.concatenate([active_order, jnp.zeros((group_size,), jnp.int32)])
    active_count = jnp.sum(flat_mask)
    rounds = (active_count + group_size - 1) // group_size

    def advance(round_index, carry):
        running_max, total_sum = carry
        picked = lax.dynamic_slice_in_dim(active_order, round_index * group_size, group_size)
        live_slot = (
            round_index * group_size + jnp.arange(group_size, dtype=jnp.int32) < active_count
        )
        row_pick = picked // col_span
        col_pick = picked % col_span
        row_tiles = jnp.take(row_blocks, row_pick, axis=1)
        col_tiles = jnp.take(col_blocks, col_pick, axis=1)
        inner_tiles = jnp.einsum(
            "dgr,dgc->grc", row_tiles, col_tiles, preferred_element_type=jnp.float32
        )
        tile_cost = row_sq[row_pick][:, :, None] + col_sq[col_pick][:, None, :] - 2.0 * inner_tiles
        scores = (col_pot[col_pick][:, None, :] - tile_cost) / entropy
        row_top = jnp.where(live_slot[:, None], jnp.max(scores, axis=2), lowest)
        new_max = running_max.at[row_pick].max(row_top)
        tile_terms = jnp.sum(jnp.exp(scores - new_max[row_pick][:, :, None]), axis=2)
        tile_terms = jnp.where(live_slot[:, None], tile_terms, 0.0)
        rescaled = total_sum * jnp.exp(running_max - new_max)
        return (new_max, rescaled.at[row_pick].add(tile_terms))

    start_max = jnp.full((row_span, block_width), lowest, jnp.float32)
    start_sum = jnp.zeros((row_span, block_width), jnp.float32)
    return lax.fori_loop(0, rounds, advance, (start_max, start_sum))


def finish(logmass, row_top, row_total):
    return entropy * logmass - entropy * (row_top + jnp.log(row_total))


def source_side(local_max, local_total, logmass):
    row_top = lax.pmax(local_max, "tgt")
    row_sums = lax.psum(local_total * jnp.exp(local_max - row_top), "tgt")
    return finish(logmass, row_top, row_sums)


def target_side(local_max, local_total, logmass):
    col_top = lax.pmax(local_max, "src")
    col_sums = lax.psum(local_total * jnp.exp(local_max - col_top), "src")
    return finish(logmass, col_top, col_sums)


def local(src_cells, tgt_cells, src_logmass, tgt_logmass, init_potential, pattern):
    src_sq = jnp.sum(jnp.square(src_cells.astype(jnp.float32)), axis=0).reshape(-1, BLOCK)
    tgt_sq = jnp.sum(jnp.square(tgt_cells.astype(jnp.float32)), axis=0).reshape(-1, BLOCK)
    flipped = pattern.T
    tgt_pot = init_potential
    src_pot = jnp.zeros_like(src_logmass)
    for sweep_index in range(SWEEPS):
        row_top, row_total = block_lse(
            src_cells, tgt_cells, src_sq, tgt_sq, tgt_pot.reshape(-1, BLOCK), pattern
        )
        src_pot = source_side(row_top.reshape(-1), row_total.reshape(-1), src_logmass)
        col_top, col_total = block_lse(
            tgt_cells, src_cells, tgt_sq, src_sq, src_pot.reshape(-1, BLOCK), flipped
        )
        tgt_pot = target_side(col_top.reshape(-1), col_total.reshape(-1), tgt_logmass)
    return (src_pot, tgt_pot)


def solution(mesh):
    return jax.shard_map(
        local,
        mesh=mesh,
        in_specs=(P(None, "src"), P(None, "tgt"), P("src"), P("tgt"), P("tgt"), P("src", "tgt")),
        out_specs=(P("src"), P("tgt")),
        check_vma=False,
    )
```

profile of v0, /device:TPU:8, one launch (start us, length us, event | category | flops | bytes accessed | tf_op | source)
XLA Modules:
  0.0 1083.8 jit_solution(2073602724318638158)
XLA Ops:
  19.6 69.6 %while.56 = (s32[]{:T(128)}, f32[32,512]{1,0:T(8,128)S(1)}, f32[32,512]{1,0:T(8,128)S(1)}, s32[]{:T(128)}, s32[264]{0:T(512)S(1)}, /*index=5*/s32[]{:T(128)}, f3...) while((s32[]{:T(128)}, f32[32,512]{1,0:T(8,128)S(1)}, ...), condition=%wide.region_11.14_spmd, body=%wide.region_6.13_spmd.sunk | while | flops 296266016 | bytes 20899496 | solution.py:53
  24.1 5.5 fusion.88
  31.0 5.2 exponential_reduce_fusion.8
  41.5 5.5 fusion.88
  58.9 5.5 fusion.88
  76.3 5.5 fusion.88
  83.1 5.2 exponential_reduce_fusion.8
  90.0 175.6 %all-reduce.7.cloned.1.call-done = f32[16384]{0:T(1024)} async-done(((f32[16384]{0:T(1024)}), f32[16384]{0:T(1024)}) %all-reduce.7.cloned.1.call-update) | async-done | bytes 65552 | tf_op jit(solution)/shard_map/pmax | solution.py:61
  271.1 103.1 %all-reduce.9.cloned.1.call-done = f32[16384]{0:T(1024)} async-done(((f32[16384]{0:T(1024)}), f32[16384]{0:T(1024)}) %all-reduce.9.cloned.1.call-update) | async-done | bytes 65552 | tf_op jit(solution)/shard_map/psum | solution.py:62
  375.1 69.1 %while.57 = (s32[]{:T(128)}, f32[8,512]{1,0:T(8,128)S(1)}, f32[8,512]{1,0:T(8,128)S(1)}, s32[]{:T(128)}, s32[264]{0:T(512)S(1)}, /*index=5*/s32[]{:T(128)}, f32[...) while((s32[]{:T(128)}, f32[8,512]{1,0:T(8,128)S(1)}, ...), condition=%wide.region_19.22_spmd, body=%wide.region_14.21_spmd.sunk | while | flops 296241440 | bytes 20407976 | solution.py:53
  379.7 5.5 fusion.91
  386.4 5.2 exponential_reduce_fusion.9
  396.9 5.5 fusion.91
  403.7 5.2 exponential_reduce_fusion.9
  414.2 5.5 fusion.91
  431.5 5.5 fusion.91
  444.3 61.4 %pmax.29 = f32[4096]{0:T(1024)S(1)} all-reduce(f32[4096]{0:T(1024)S(1)} %bitcast.100), channel_id=1, replica_groups=mesh['src'=8,'tgt'=32] {'src'}, use_global_device_ids=true, to_apply=%region_20.23 | all-reduce | flops 4096 | bytes 32768 | tf_op jit(solution)/shard_map/pmax | solution.py:67
  505.7 27.6 %psum.29 = f32[4096]{0:T(1024)S(1)} all-reduce(f32[4096]{0:T(1024)S(1)} %exponential_multiply_fusion.7), channel_id=1, replica_groups=mesh['src'=8,'tgt'=32] {'src'}, use_global_device_ids=true, to_apply=%region_21.24 | all-reduce | flops 4096 | bytes 32768 | tf_op jit(solution)/shard_map/psum | solution.py:68
  533.4 69.7 %while.58 = (s32[]{:T(128)}, f32[32,512]{1,0:T(8,128)S(1)}, f32[32,512]{1,0:T(8,128)S(1)}, s32[]{:T(128)}, s32[264]{0:T(512)S(1)}, /*index=5*/s32[]{:T(128)}, f3...) while((s32[]{:T(128)}, f32[32,512]{1,0:T(8,128)S(1)}, ...), condition=%wide.region_27.30_spmd, body=%wide.region_22.29_spmd.sunk | while | flops 296266016 | bytes 20899496 | solution.py:53
  538.0 5.5 fusion.94
  555.4 5.5 fusion.94
  572.8 5.5 fusion.94
  590.2 5.5 fusion.94
  603.9 204.4 %all-reduce.11.cloned.1.call-done = f32[16384]{0:T(1024)} async-done(((f32[16384]{0:T(1024)}), f32[16384]{0:T(1024)}) %all-reduce.11.cloned.1.call-update) | async-done | bytes 65552 | tf_op jit(solution)/shard_map/pmax | solution.py:61
  809.8 107.1 %all-reduce.13.cloned.1.call-done = f32[16384]{0:T(1024)} async-done(((f32[16384]{0:T(1024)}), f32[16384]{0:T(1024)}) %all-reduce.13.cloned.1.call-update) | async-done | bytes 65552 | tf_op jit(solution)/shard_map/psum | solution.py:62
  918.5 69.1 %while.59 = (s32[]{:T(128)}, f32[8,512]{1,0:T(8,128)S(1)}, f32[8,512]{1,0:T(8,128)S(1)}, s32[]{:T(128)}, s32[264]{0:T(512)S(1)}, /*index=5*/s32[]{:T(128)}, f32[...) while((s32[]{:T(128)}, f32[8,512]{1,0:T(8,128)S(1)}, ...), condition=%wide.region_35.38_spmd, body=%wide.region_30.37_spmd.sunk | while | flops 296241440 | bytes 20407976 | solution.py:53
  923.0 5.5 fusion.97
  940.2 5.5 fusion.97
  957.5 5.5 fusion.97
  974.8 5.5 fusion.97
  987.6 61.4 %pmax.31 = f32[4096]{0:T(1024)S(1)} all-reduce(f32[4096]{0:T(1024)S(1)} %bitcast.102), channel_id=1, replica_groups=mesh['src'=8,'tgt'=32] {'src'}, use_global_device_ids=true, to_apply=%region_36.39 | all-reduce | flops 4096 | bytes 32768 | tf_op jit(solution)/shard_map/pmax | solution.py:67
  1049.0 27.6 %psum.31 = f32[4096]{0:T(1024)S(1)} all-reduce(f32[4096]{0:T(1024)S(1)} %exponential_multiply_fusion.6), channel_id=1, replica_groups=mesh['src'=8,'tgt'=32] {'src'}, use_global_device_ids=true, to_apply=%region_37.40 | all-reduce | flops 4096 | bytes 32768 | tf_op jit(solution)/shard_map/psum | solution.py:68
  (310 shorter events, 189.5 us)
Async XLA Ops:
  7.2 258.5 %all-reduce.7.cloned.1.call-start = ((), (), s32[]{:S(2)}) async-start(), calls=%async_computation | async-start | bytes 131072 | tf_op jit(solution)/shard_map/pmax | solution.py:61
  89.9 284.3 %all-reduce.9.cloned.1.call-start = ((), (), s32[]{:S(2)}) async-start(), calls=%async_computation.1 | async-start | bytes 131072 | tf_op jit(solution)/shard_map/psum | solution.py:62
  267.2 541.0 %all-reduce.11.cloned.1.call-start = ((), (), s32[]{:S(2)}) async-start(), calls=%async_computation.2 | async-start | bytes 131072 | tf_op jit(solution)/shard_map/pmax | solution.py:61
  375.1 158.2 %copy-start.1 = (f32[4096]{0:T(1024)S(1)}, f32[4096]{0:T(1024)}, u32[]{:S(2)}) copy-start(f32[4096]{0:T(1024)} %param.21) | copy-start | bytes 49156
  603.8 313.1 %all-reduce.13.cloned.1.call-start = ((), (), s32[]{:S(2)}) async-start(), calls=%async_computation.3 | async-start | bytes 131072 | tf_op jit(solution)/shard_map/psum | solution.py:62
  917.8 0.6 copy-start
Sparse Core Ops, SparseCore 0:
  90.0 175.6 all-reduce.6
  269.5 104.6 all-reduce.8
  603.9 204.2 all-reduce.10
  812.3 104.6 all-reduce.12
where the time goes:
time: 1090 us; the launch traced here: 1080 us
  waiting for transfers between devices  590 us (54%)
  blocking collectives  178 us (16%)
  other arithmetic  136 us (12%)
  matrix products  87.9 us (8%)
  local copies, waits for them, and re-layouts  74.2 us (7%)
  between operations  15.3 us (1%)
    pmax x2, waiting for transfers between devices, source_side(): row_top = lax.pmax(local_max, 'tgt')  380 us
    psum x2, waiting for transfers between devices, source_side(): row_sums = lax.psum(local_total * jnp.exp(local_max - row_top), 'tgt')  210 us
    pmax x2, blocking collectives, target_side(): col_top = lax.pmax(local_max, 'src')  123 us
    dot_general x16, matrix products, advance(): jnp.einsum('dgr,dgc->grc', row_tiles, col_tiles, preferred_element_type=j...  87.9 us
    reduce_sum x16, other arithmetic, advance(): jnp.sum(jnp.exp(scores - new_max[row_pick][:, :, None]), axis=2)  83.5 us
    psum x2, blocking collectives, target_side(): col_sums = lax.psum(local_total * jnp.exp(local_max - col_top), 'src')  55.2 us
    gather x16, local copies, waits for them, and re-layouts, advance(): col_tiles = jnp.take(col_blocks, col_pick, axis=1)  22.8 us
  transfers between devices with their start and end apart: 4, of which 4 were waited for; matrix products, arithmetic and copies ran while one was open for 0% of the time, Pallas kernels for 0%

commit v1 on v0

v1 whole, which is shorter than its diff:
```python
import jax
import jax.numpy as jnp
from jax import lax
from jax.experimental import pallas as pl
from jax.experimental.pallas import tpu as pltpu
from jax.sharding import PartitionSpec as P

BLOCK = 512
LANES = 128
PARTS = BLOCK // LANES
SWEEPS = 2
ENTROPY = 0.5
LOWEST = -1e30
GROUP = 8
VMEM_LIMIT = 40 << 20


def list_pairs(pattern_ref, list_ref):
    cols, rows = pattern_ref.shape
    count = jnp.int32(0)
    for row in range(rows):
        for col in range(cols):
            list_ref[count] = row * cols + col
            count = count + pattern_ref[col, row]
    for extra in range(GROUP):
        list_ref[count + extra] = rows * cols
    list_ref[rows * cols + GROUP] = count


def blocks_of(ref):
    rows = ref.shape[0] // PARTS
    return jnp.concatenate([ref[pl.ds(part, rows, stride=PARTS), :] for part in range(PARTS)], axis=1)


def store_blocks(ref, values):
    rows = values.shape[0]
    for part in range(PARTS):
        ref[pl.ds(part, rows, stride=PARTS), :] = values[:, part * LANES : (part + 1) * LANES]


def factors(potential, reach):
    shift = jnp.max(potential)
    extent = shift - jnp.min(potential)
    safe = jnp.logical_and(reach <= 70.0, reach + extent <= 80.0)
    below = potential - shift
    return jnp.where(safe, jnp.exp(below), below), shift, safe


def log_or_lowest(total, top):
    some = total > 0.0
    return jnp.where(some, jnp.log(jnp.where(some, total, 1.0)) + top, LOWEST)


def run_pairs(list_ref, visit):
    count = list_ref[list_ref.shape[0] - 1]

    def turn(width, base):
        def body(step, carry):
            for at in range(width):
                visit(list_ref[base + step * width + at])
            return carry

        return body

    full = lax.div(count, GROUP)
    lax.fori_loop(0, full, turn(GROUP, 0), 0)
    lax.fori_loop(0, lax.div(count - full * GROUP + 1, 2), turn(2, full * GROUP), 0)


def run_pairs_singly(list_ref, visit):
    def body(step, carry):
        visit(list_ref[step])
        return carry

    lax.fori_loop(0, list_ref[list_ref.shape[0] - 1], body, 0)


def place(pair, rows, cols):
    return lax.rem(lax.div(pair, cols), rows), lax.rem(pair, cols)


def tile_of(tall_ref, src_ref, src_block, tgt_block, start=0, size=BLOCK):
    left = tall_ref[pl.ds(pl.multiple_of(tgt_block * BLOCK + start, size), size), :]
    right = src_ref[:, pl.ds(pl.multiple_of(src_block * BLOCK, BLOCK), BLOCK)]
    return jnp.dot(left, right, preferred_element_type=jnp.float32)


def lane_part(values, part):
    return values[:, part * LANES : (part + 1) * LANES]


def fold_lanes(values, fold):
    out = lane_part(values, 0)
    for part in range(1, PARTS):
        out = fold(out, lane_part(values, part))
    return out


def spread_down(weights, spread_ref):
    for row in range(weights.shape[0]):
        down = jnp.broadcast_to(weights[row : row + 1, :], (LANES, LANES)).T
        spread_ref[row * LANES : (row + 1) * LANES, :] = down


def src_sums(potential, reach, list_ref, tall_ref, src_ref, spread_ref, sum_ref, top_ref, out_ref):
    rows, cols = src_ref.shape[1] // BLOCK, tall_ref.shape[0] // BLOCK
    weights, shift, safe = factors(potential, reach)
    spread_down(weights, spread_ref)
    sum_ref[...] = jnp.zeros_like(sum_ref)

    @pl.when(safe)
    def _():
        def visit(pair):
            src_block, tgt_block = place(pair, rows, cols)
            tile = jnp.exp(tile_of(tall_ref, src_ref, src_block, tgt_block))
            down = spread_ref[pl.ds(pl.multiple_of(tgt_block * BLOCK, BLOCK), BLOCK), :]
            sums = [
                (lane_part(tile, part) * down).reshape(-1, 8, LANES).sum(0) for part in range(PARTS)
            ]
            sum_ref[lax.div(pair, cols)] += jnp.concatenate(sums, axis=1)

        run_pairs(list_ref, visit)
        store_blocks(out_ref, log_or_lowest(sum_ref[0:rows].sum(1), shift))

    @pl.when(jnp.logical_not(safe))
    def _():
        top_ref[...] = jnp.full_like(top_ref, LOWEST)

        def visit(pair):
            src_block, tgt_block = place(pair, rows, cols)

            def chunk(index, carry):
                start = pl.multiple_of(index * LANES, LANES)
                down = spread_ref[pl.ds(pl.multiple_of(tgt_block * BLOCK + start, LANES), LANES), :]
                tile = tile_of(tall_ref, src_ref, src_block, tgt_block, start, LANES)
                tile = (tile + jnp.concatenate([down] * PARTS, axis=1)).reshape(-1, 8, BLOCK)
                old = top_ref[src_block]
                new = jnp.maximum(old, tile.max(0))
                more = jnp.exp(tile - new[None]).sum(0)
                sum_ref[src_block] = sum_ref[src_block] * jnp.exp(old - new) + more
                top_ref[src_block] = new
                return carry

            lax.fori_loop(0, PARTS, chunk, 0)

        run_pairs_singly(list_ref, visit)
        slots = top_ref[0:rows]
        top = slots.max(1, keepdims=True)
        total = (sum_ref[0:rows] * jnp.exp(slots - top)).sum(1)
        store_blocks(out_ref, log_or_lowest(total, top[:, 0] + shift))


def tgt_sums(potential, reach, list_ref, tall_ref, src_ref, weight_ref, sum_ref, top_ref, out_ref):
    rows, cols = src_ref.shape[1] // BLOCK, tall_ref.shape[0] // BLOCK
    weights, shift, safe = factors(potential, reach)
    weight_ref[...] = weights
    sum_ref[...] = jnp.zeros_like(sum_ref)

    def store(block, total, top):
        values = log_or_lowest(total, top)
        for part in range(PARTS):
            at = block * PARTS + part
            out_ref[0, at : at + 1, :] = lane_part(values, part)

    @pl.when(safe)
    def _():
        def visit(pair):
            src_block, tgt_block = place(pair, rows, cols)
            at = jnp.where(pair < rows * cols, tgt_block, cols)
            tile = jnp.exp(tile_of(tall_ref, src_ref, src_block, tgt_block))
            sum_ref[at] += fold_lanes(tile * weight_ref[pl.ds(src_block, 1), :], jnp.add)

        run_pairs(list_ref, visit)
        for block in range(cols):
            store(block, sum_ref[block].T.sum(0, keepdims=True), shift)

    @pl.when(jnp.logical_not(safe))
    def _():
        top_ref[...] = jnp.full_like(top_ref, LOWEST)

        def visit(pair):
            src_block, tgt_block = place(pair, rows, cols)
            right = weight_ref[pl.ds(src_block, 1), :]

            def chunk(index, carry):
                start = pl.multiple_of(index * LANES, LANES)
                tile = tile_of(tall_ref, src_ref, src_block, tgt_block, start, LANES) + right
                at = (tgt_block, pl.ds(start, LANES), slice(None))
                old = top_ref[at]
                new = jnp.maximum(old, fold_lanes(tile, jnp.maximum))
                more = fold_lanes(jnp.exp(tile - jnp.concatenate([new] * PARTS, axis=1)), jnp.add)
                sum_ref[at] = sum_ref[at] * jnp.exp(old - new) + more
                top_ref[at] = new
                return carry

            lax.fori_loop(0, PARTS, chunk, 0)

        run_pairs_singly(list_ref, visit)
        for block in range(cols):
            slots = top_ref[block].T
            top = slots.max(0, keepdims=True)
            total = (sum_ref[block].T * jnp.exp(slots - top)).sum(0, keepdims=True)
            store(block, total, top + shift)

    for copy in range(1, out_ref.shape[0]):
        out_ref[copy] = out_ref[0]


def store_squares(cells_ref, out_ref):
    for block in range(cells_ref.shape[1] // BLOCK):
        cells = cells_ref[:, block * BLOCK : (block + 1) * BLOCK].astype(jnp.float32)
        squares = jnp.sum(cells * cells, axis=0, keepdims=True)
        for part in range(PARTS):
            at = block * PARTS + part
            out_ref[at : at + 1, :] = lane_part(squares, part)


def first_src_kernel(
    pattern_hbm, src_hbm, tgt_hbm, pot_hbm,
    out_ref, src_ref, src_sq_ref, tgt_sq_ref, reach_ref, tall_ref, list_ref,
    pattern_ref, tgt_ref, pot_ref, sems, spread_ref, sum_ref, top_ref,
):
    pattern_copy, tgt_copy, pot_copy, src_copy = copies = [
        pltpu.make_async_copy(source, target, sems.at[at])
        for at, (source, target) in enumerate(
            [(pattern_hbm, pattern_ref), (tgt_hbm, tgt_ref), (pot_hbm, pot_ref), (src_hbm, src_ref)]
        )
    ]
    for copy in copies:
        copy.start()
    pattern_copy.wait()
    list_pairs(pattern_ref, list_ref)
    tgt_copy.wait()
    for block in range(tgt_ref.shape[1] // BLOCK):
        cells = tgt_ref[:, block * BLOCK : (block + 1) * BLOCK].astype(jnp.float32) * 4.0
        tall_ref[block * BLOCK : (block + 1) * BLOCK, :] = cells.T.astype(jnp.bfloat16)
    store_squares(tgt_ref, tgt_sq_ref)
    pot_copy.wait()
    src_copy.wait()
    store_squares(src_ref, src_sq_ref)
    reach = 4.0 * jnp.sqrt(jnp.max(src_sq_ref[...], keepdims=True)) * jnp.sqrt(
        jnp.max(tgt_sq_ref[...], keepdims=True)
    )
    reach_ref[...] = jnp.broadcast_to(reach, reach_ref.shape)
    potential = 2.0 * (pot_ref[...] - tgt_sq_ref[...])
    src_sums(
        potential, jnp.max(reach), list_ref, tall_ref, src_ref, spread_ref, sum_ref, top_ref, out_ref
    )


def src_kernel(
    list_ref, src_ref, tall_ref, gathered_ref, mass_ref, reach_ref,
    out_ref,
    spread_ref, sum_ref, top_ref,
):
    gathered = gathered_ref[...]
    top = gathered.max(0)
    potential = mass_ref[...] - (top + jnp.log(jnp.exp(gathered - top[None]).sum(0)))
    src_sums(
        potential, jnp.max(reach_ref[...]), list_ref, tall_ref, src_ref, spread_ref, sum_ref, top_ref,
        out_ref,
    )


def tgt_kernel(
    list_ref, src_ref, tall_ref, logs_ref, mass_ref, reach_ref,
    out_ref,
    weight_ref, sum_ref, top_ref,
):
    potential = blocks_of(mass_ref) - blocks_of(logs_ref)
    tgt_sums(
        potential, jnp.max(reach_ref[...]), list_ref, tall_ref, src_ref, weight_ref, sum_ref, top_ref,
        out_ref,
    )


def last_tgt_kernel(
    list_ref, src_ref, tall_ref, logs_ref, mass_ref, reach_ref, src_sq_ref,
    out_ref, src_pot_hbm,
    weight_ref, sum_ref, top_ref, src_pot_ref, sem,
):
    src_pot_ref[...] = src_sq_ref[...] + ENTROPY * (mass_ref[...] - logs_ref[...])
    copy = pltpu.make_async_copy(src_pot_ref, src_pot_hbm, sem)
    copy.start()
    tgt_kernel(
        list_ref, src_ref, tall_ref, logs_ref, mass_ref, reach_ref, out_ref, weight_ref, sum_ref, top_ref
    )
    copy.wait()


def call(kernel, args, in_spaces, outs, out_spaces, scratch, name):
    return pl.pallas_call(
        kernel,
        out_shape=outs,
        in_specs=[pl.BlockSpec(memory_space=space) for space in in_spaces],
        out_specs=[pl.BlockSpec(memory_space=space) for space in out_spaces],
        scratch_shapes=scratch,
        compiler_params=pltpu.CompilerParams(vmem_limit_bytes=VMEM_LIMIT),
        name=name,
    )(*args)


def floats(*shape):
    return jax.ShapeDtypeStruct(shape, jnp.float32)


def combine(one, other):
    top = jnp.maximum(one, other)
    return top + jnp.log(1.0 + jnp.exp(-jnp.abs(one - other)))


def over_tgt(logs):
    size = lax.axis_size("tgt")

    def from_peer(values, mask):
        return lax.ppermute(values, "tgt", [(at, at ^ mask) for at in range(size)])

    logs = combine(logs, from_peer(logs, 1))
    for stage in (2, 8):
        one, two, three = [from_peer(logs, stage * mask) for mask in (1, 2, 3)]
        top = jnp.maximum(jnp.maximum(logs, one), jnp.maximum(two, three))
        near = jnp.exp(logs - top) + jnp.exp(one - top)
        far = jnp.exp(two - top) + jnp.exp(three - top)
        logs = top + jnp.log(near + far)
    return logs


def local(src_cells, tgt_cells, src_logmass, tgt_logmass, init_potential, pattern):
    copies = lax.axis_size("src")
    depth, src_count = src_cells.shape
    tgt_count = tgt_cells.shape[1]
    rows, cols = pattern.shape
    src_shape = (src_count // LANES, LANES)
    tgt_shape = (tgt_count // LANES, LANES)
    src_mass = src_logmass.reshape(src_shape)
    tgt_mass = tgt_logmass.reshape(tgt_shape)
    vmem, smem, hbm = pltpu.VMEM, pltpu.SMEM, pltpu.HBM

    src_scratch = [
        vmem((tgt_count, LANES), jnp.float32),
        vmem((rows + 1, 8, BLOCK), jnp.float32),
        vmem((rows + 1, 8, BLOCK), jnp.float32),
    ]
    tgt_scratch = [
        vmem((rows, BLOCK), jnp.float32),
        vmem((cols + 1, BLOCK, LANES), jnp.float32),
        vmem((cols + 1, BLOCK, LANES), jnp.float32),
    ]
    logs, src_held, src_sq, tgt_sq, reach, tall, pairs = call(
        first_src_kernel,
        [
            pltpu.with_memory_space_constraint(array, hbm)
            for array in (pattern.T, src_cells, tgt_cells, init_potential.reshape(tgt_shape))
        ],
        [hbm] * 4,
        [
            floats(*src_shape), jax.ShapeDtypeStruct(src_cells.shape, src_cells.dtype),
            floats(*src_shape), floats(*tgt_shape), floats(8, LANES),
            jax.ShapeDtypeStruct((tgt_count, depth), jnp.bfloat16),
            jax.ShapeDtypeStruct((rows * cols + GROUP + 1,), jnp.int32),
        ],
        [vmem] * 6 + [smem],
        [
            smem((cols, rows), jnp.int32), vmem(tgt_cells.shape, tgt_cells.dtype),
            vmem(tgt_shape, jnp.float32), pltpu.SemaphoreType.DMA((4,)),
        ] + src_scratch,
        "src_first",
    )
    for sweep in range(SWEEPS):
        if sweep:
            (logs,) = call(
                src_kernel, [pairs, src_held, tall, gathered, tgt_mass, reach], [smem] + [vmem] * 5,
                [floats(*src_shape)], [vmem], src_scratch, "src_next",
            )
        src_logs = over_tgt(logs)
        args = [pairs, src_held, tall, src_logs, src_mass, reach]
        if sweep < SWEEPS - 1:
            (logs,) = call(
                tgt_kernel, args, [smem] + [vmem] * 5, [floats(copies, *tgt_shape)], [vmem],
                tgt_scratch, "tgt",
            )
        else:
            logs, src_pot = call(
                last_tgt_kernel, args + [src_sq], [smem] + [vmem] * 6,
                [floats(copies, *tgt_shape), floats(*src_shape)], [vmem, hbm],
                tgt_scratch + [vmem(src_shape, jnp.float32), pltpu.SemaphoreType.DMA], "tgt_last",
            )
        gathered = lax.all_to_all(logs, "src", 0, 0)
    top = gathered.max(0)
    tgt_logs = top + jnp.log(jnp.exp(gathered - top[None]).sum(0))
    tgt_pot = tgt_sq + ENTROPY * (tgt_mass - tgt_logs)
    return src_pot.reshape(-1), tgt_pot.reshape(-1)


def solution(mesh):
    return jax.shard_map(
        local,
        mesh=mesh,
        in_specs=(P(None, "src"), P(None, "tgt"), P("src"), P("tgt"), P("tgt"), P("src", "tgt")),
        out_specs=(P("src"), P("tgt")),
        check_vma=False,
    )
```

time: 1090 us -> 246 us (0.23)
  waiting for transfers between devices: 590 us -> 14.6 us
  other arithmetic: 136 us -> 0.99 us
  blocking collectives: 178 us -> 67 us
  Pallas kernels: 0 us -> 104 us
  matrix products: 87.9 us -> 0 us
  local copies, waits for them, and re-layouts: 74.2 us -> 0.01 us
  starting transfers between devices: 0.16 us -> 56.3 us
  between operations: 15.3 us -> 0.77 us
    pmax x2 -> x0, waiting for transfers between devices: 380 us -> none  [source_side(): row_top = lax.pmax(local_max, 'tgt')]
    psum x2 -> x0, waiting for transfers between devices: 210 us -> none  [source_side(): row_sums = lax.psum(local_total * jnp.exp(local_max - row_top), 'tgt')]
    pmax x2 -> x0, blocking collectives: 123 us -> none  [target_side(): col_top = lax.pmax(local_max, 'src')]
    pallas_call x0 -> x4, Pallas kernels: none -> 104 us  [call(): pl.pallas_call(kernel, out_shape=outs, in_specs=[pl.BlockSpec(memory_spac...]
    reduce_sum x19 -> x1, other arithmetic: 88.2 us -> 0.03 us  [local(): tgt_logs = top + jnp.log(jnp.exp(gathered - top[None]).sum(0))]
    dot_general x16 -> x0, matrix products: 87.9 us -> none  [advance(): jnp.einsum('dgr,dgc->grc', row_tiles, col_tiles, preferred_element_type=j...]
    gather x96 -> x0, local copies, waits for them, and re-layouts: 68.1 us -> none  [the longest x16 22.8 us: advance(): col_tiles = jnp.take(col_blocks, col_pick, axis=1)]
    all_to_all x0 -> x2, blocking collectives: none -> 67 us  [local(): gathered = lax.all_to_all(logs, 'src', 0, 0)]
  transfers between devices with their start and end apart: 4 -> 14, of which waited for: 4 -> 12; matrix products, arithmetic and copies ran while one was open for 0% -> 0% of each run, Pallas kernels for 0% -> 0%
where the time goes in v1:
time: 246 us; the launch traced here: 243 us
  Pallas kernels  104 us (42%)
  blocking collectives  67 us (27%)
  starting transfers between devices  56.3 us (23%)
  waiting for transfers between devices  14.6 us (6%)
    pallas_call x4, Pallas kernels, call(): pl.pallas_call(kernel, out_shape=outs, in_specs=[pl.BlockSpec(memory_spac...  104 us
    all_to_all x2, blocking collectives, local(): gathered = lax.all_to_all(logs, 'src', 0, 0)  67 us
    ppermute x14, starting transfers between devices, from_peer(): return lax.ppermute(values, 'tgt', [(at, at ^ mask) for at in range(size)])  56.3 us
    ppermute x14, waiting for transfers between devices, from_peer(): return lax.ppermute(values, 'tgt', [(at, at ^ mask) for at in range(size)])  14.6 us
  transfers between devices with their start and end apart: 14, of which 12 were waited for; matrix products, arithmetic and copies ran while one was open for 0% of the time, Pallas kernels for 0%

profile of v1, /device:TPU:8, one launch (start us, length us, event | category | flops | bytes accessed | tf_op | source)
XLA Modules:
  0.0 243.5 jit_solution(7243675133169082383)
XLA Ops:
  0.6 28.2 %src_first.1 = (f32[128,128]{1,0:T(8,128)S(1)}, bf16[64,16384]{1,0:T(8,128)(2,1)S(1)}, f32[128,128]{1,0:T(8,128)S(1)}, f32[32,128]{1,0:T(8,128)S(1)}, f32[8,128]...) custom-call(s32[8,32]{1,0:T(8,128)} %bitcast.12, bf16[64,16384]{1,0:T(8,128)(2,1)} %src_hbm.1, ...), custom_call_target="tpu_custom_call" | custom-call | tf_op jit(solution)/shard_map/src_first/pallas_call | solution.py:292
  28.9 17.2 %collective-permute-start = (f32[128,128]{1,0:T(8,128)S(1)}, f32[128,128]{1,0:T(8,128)S(1)}, u32[]{:S(2)}, u32[]{:S(2)}) collective-permute-start(f32[128,128]{1,0:T(8,128)S(1)} %get-tuple-element.14), channel_id=1, source_target_pairs={{0,1},{1,0},{2,3},{3,2},{4,5},{5,4},{6,7},{7,6},{8,9},{9,8},{10,11... | collective-permute-start | bytes 196616 | tf_op jit(solution)/shard_map/ppermute | solution.py:316
  46.1 0.9 collective-permute-done
  47.0 0.1 collective-permute-start.3
  47.1 0.1 collective-permute-start.2
  47.2 4.0 %collective-permute-start.1 = (f32[128,128]{1,0:T(8,128)S(1)}, f32[128,128]{1,0:T(8,128)S(1)}, u32[]{:S(2)}, u32[]{:S(2)}) collective-permute-start(f32[128,128]{1,0:T(8,128)S(1)} %log_add_fusion.5), channel_id=1, source_target_pairs={{0,2},{1,3},{2,0},{3,1},{4,6},{5,7},{6,4},{7,5},{8,10},{9,11},{10,... | collective-permute-start | bytes 196616 | tf_op jit(solution)/shard_map/ppermute | solution.py:316
  51.2 2.9 %collective-permute-done.3 = f32[128,128]{1,0:T(8,128)S(1)} collective-permute-done((f32[128,128]{1,0:T(8,128)S(1)}, f32[128,128]{1,0:T(8,128)S(1)}, u32[]{:S(2)}, u32[]{:S(2)}) %collective-permute-start.3) | collective-permute-done | bytes 65568 | tf_op jit(solution)/shard_map/ppermute | solution.py:316
  54.1 0.6 collective-permute-done.1
  54.7 0.1 collective-permute-start.6
  54.8 1.8 collective-permute-start.5
  56.6 2.3 collective-permute-start.4
  58.9 0.7 collective-permute-done.6
  59.7 1.0 collective-permute-done.5
  60.7 1.2 collective-permute-done.4
  61.9 24.7 %tgt.1 = f32[8,32,128]{2,1,0:T(8,128)S(1)} custom-call(s32[265]{0:T(512)S(1)} %get-tuple-element.11.list_ref, bf16[64,16384]{1,0:T(8,128)(2,1)S(1)} %get-tuple-element.12.src_ref, bf16[4096,64]{1,0:T(8,128)(2,1)S(1)} %get-tuple-element.13.tall_ref, f32[128,128]{1,0:T(8,128)S(1)} %log_add_fusion.3.logs_ref, f32[128,128]{1,0:T(8,128)S(1)} %bitcast.8, ...), custom_call_target="tpu_custom_call" | custom-call | tf_op jit(solution)/shard_map/tgt/pallas_call | solution.py:292
  86.6 33.5 %all_to_all.10.gathered_ref = f32[8,32,128]{2,1,0:T(8,128)S(1)} all-to-all(f32[8,32,128]{2,1,0:T(8,128)S(1)} %tgt.1), channel_id=1, replica_groups=mesh['src'=8,'tgt'=32] {'src'}, dimensions={0} | all-to-all | bytes 262144 | tf_op jit(solution)/shard_map/all_to_all | solution.py:388
  120.1 26.1 %src_next.1 = f32[128,128]{1,0:T(8,128)S(1)} custom-call(s32[265]{0:T(512)S(1)} %get-tuple-element.11.list_ref, bf16[64,16384]{1,0:T(8,128)(2,1)S(1)} %get-tuple-element.12.src_ref, bf16[4096,64]{1,0:T(8,128)(2,1)S(1)} %get-tuple-element.13.tall_ref, f32[8,32,128]{2,1,0:T(8,128)S(1)} %all_to_all.10.gathered_ref, f32[32,128]{1,0:T(8,128)S(1)} %bitcast.10, ...), custom_call_target="tpu_custom_call" | custom-call | tf_op jit(solution)/shard_map/src_next/pallas_call | solution.py:292
  146.2 22.4 %collective-permute-start.7 = (f32[128,128]{1,0:T(8,128)S(1)}, f32[128,128]{1,0:T(8,128)S(1)}, u32[]{:S(2)}, u32[]{:S(2)}) collective-permute-start(f32[128,128]{1,0:T(8,128)S(1)} %src_next.1), channel_id=1, source_target_pairs={{0,1},{1,0},{2,3},{3,2},{4,5},{5,4},{6,7},{7,6},{8,9},{9,8},{10,11... | collective-permute-start | bytes 196616 | tf_op jit(solution)/shard_map/ppermute | solution.py:316
  168.7 0.9 collective-permute-done.7
  169.6 0.1 collective-permute-start.10
  169.7 0.1 collective-permute-start.9
  169.8 4.0 %collective-permute-start.8 = (f32[128,128]{1,0:T(8,128)S(1)}, f32[128,128]{1,0:T(8,128)S(1)}, u32[]{:S(2)}, u32[]{:S(2)}) collective-permute-start(f32[128,128]{1,0:T(8,128)S(1)} %log_add_fusion.2), channel_id=1, source_target_pairs={{0,2},{1,3},{2,0},{3,1},{4,6},{5,7},{6,4},{7,5},{8,10},{9,11},{10,... | collective-permute-start | bytes 196616 | tf_op jit(solution)/shard_map/ppermute | solution.py:316
  173.8 2.9 %collective-permute-done.10 = f32[128,128]{1,0:T(8,128)S(1)} collective-permute-done((f32[128,128]{1,0:T(8,128)S(1)}, f32[128,128]{1,0:T(8,128)S(1)}, u32[]{:S(2)}, u32[]{:S(2)}) %collective-permute-start.10) | collective-permute-done | bytes 65568 | tf_op jit(solution)/shard_map/ppermute | solution.py:316
  176.7 0.6 collective-permute-done.8
  177.4 0.1 collective-permute-start.12
  177.5 4.0 %collective-permute-start.11 = (f32[128,128]{1,0:T(8,128)S(1)}, f32[128,128]{1,0:T(8,128)S(1)}, u32[]{:S(2)}, u32[]{:S(2)}) collective-permute-start(f32[128,128]{1,0:T(8,128)S(1)} %log_add_fusion.1), channel_id=1, source_target_pairs={{0,8},{1,9},{2,10},{3,11},{4,12},{5,13},{6,14},{7,15},{8,0},{9,1},... | collective-permute-start | bytes 196616 | tf_op jit(solution)/shard_map/ppermute | solution.py:316
  181.5 0.7 collective-permute-done.13
  182.2 1.0 collective-permute-done.12
  183.3 1.2 collective-permute-done.11
  184.5 24.7 %tgt_last.1 = (f32[8,32,128]{2,1,0:T(8,128)S(1)}, f32[128,128]{1,0:T(8,128)}) custom-call(s32[265]{0:T(512)S(1)} %get-tuple-element.11.list_ref, bf16[64,16384]{1,0:T(8,128)(2,1)S(1)} %get-tuple-element.12.src_ref, bf16[4096,64]{1,0:T(8,128)(2,1)S(1)} %get-tuple-element.13.tall_ref, f32[128,128]{1,0:T(8,128)S(1)} %log_add_fusion.logs_ref, ...), custom_call_target="tpu_custom_call" | custom-call | tf_op jit(solution)/shard_map/tgt_last/pallas_call | solution.py:292
  209.2 33.5 %all_to_all.11 = f32[8,32,128]{2,1,0:T(8,128)S(1)} all-to-all(f32[8,32,128]{2,1,0:T(8,128)S(1)} %get-tuple-element.19), channel_id=1, replica_groups=mesh['src'=8,'tgt'=32] {'src'}, dimensions={0} | all-to-all | bytes 262144 | tf_op jit(solution)/shard_map/all_to_all | solution.py:388
  242.8 0.6 add_bitcast_fusion
  (15 shorter events, 0.5 us)
Async XLA Ops:
  0.6 61.3 %copy-start = (f32[16384]{0:T(1024)S(1)}, f32[16384]{0:T(1024)}, u32[]{:S(2)}) copy-start(f32[16384]{0:T(1024)} %param.8) | copy-start | bytes 196612
  28.9 18.1 %collective-permute-start = (f32[128,128]{1,0:T(8,128)S(1)}, f32[128,128]{1,0:T(8,128)S(1)}, u32[]{:S(2)}, u32[]{:S(2)}) collective-permute-start(f32[128,128]{1,0:T(8,128)S(1)} %get-tuple-element.14), channel_id=1, source_target_pairs={{0,1},{1,0},{2,3},{3,2},{4,5},{5,4},{6,7},{7,6},{8,9},{9,8},{10,11... | collective-permute-start | bytes 196616 | tf_op jit(solution)/shard_map/ppermute | solution.py:316
  47.0 73.1 %copy-start.1 = (f32[4096]{0:T(1024)S(1)}, f32[4096]{0:T(1024)}, u32[]{:S(2)}) copy-start(f32[4096]{0:T(1024)} %param.9) | copy-start | bytes 49156
  47.0 7.1 %collective-permute-start.3 = (f32[128,128]{1,0:T(8,128)S(1)}, f32[128,128]{1,0:T(8,128)S(1)}, u32[]{:S(2)}, u32[]{:S(2)}) collective-permute-start(f32[128,128]{1,0:T(8,128)S(1)} %log_add_fusion.5), channel_id=1, source_target_pairs={{0,6},{1,7},{2,4},{3,5},{4,2},{5,3},{6,0},{7,1},{8,14},{9,15},{10,... | collective-permute-start | bytes 196616 | tf_op jit(solution)/shard_map/ppermute | solution.py:316
  47.1 7.0 %collective-permute-start.2 = (f32[128,128]{1,0:T(8,128)S(1)}, f32[128,128]{1,0:T(8,128)S(1)}, u32[]{:S(2)}, u32[]{:S(2)}) collective-permute-start(f32[128,128]{1,0:T(8,128)S(1)} %log_add_fusion.5), channel_id=1, source_target_pairs={{0,4},{1,5},{2,6},{3,7},{4,0},{5,1},{6,2},{7,3},{8,12},{9,13},{10,... | collective-permute-start | bytes 196616 | tf_op jit(solution)/shard_map/ppermute | solution.py:316
  47.2 7.4 %collective-permute-start.1 = (f32[128,128]{1,0:T(8,128)S(1)}, f32[128,128]{1,0:T(8,128)S(1)}, u32[]{:S(2)}, u32[]{:S(2)}) collective-permute-start(f32[128,128]{1,0:T(8,128)S(1)} %log_add_fusion.5), channel_id=1, source_target_pairs={{0,2},{1,3},{2,0},{3,1},{4,6},{5,7},{6,4},{7,5},{8,10},{9,11},{10,... | collective-permute-start | bytes 196616 | tf_op jit(solution)/shard_map/ppermute | solution.py:316
  54.7 4.9 %collective-permute-start.6 = (f32[128,128]{1,0:T(8,128)S(1)}, f32[128,128]{1,0:T(8,128)S(1)}, u32[]{:S(2)}, u32[]{:S(2)}) collective-permute-start(f32[128,128]{1,0:T(8,128)S(1)} %log_add_fusion.4), channel_id=1, source_target_pairs={{0,24},{1,25},{2,26},{3,27},{4,28},{5,29},{6,30},{7,31},{8,16},{9,... | collective-permute-start | bytes 196616 | tf_op jit(solution)/shard_map/ppermute | solution.py:316
  54.8 5.9 %collective-permute-start.5 = (f32[128,128]{1,0:T(8,128)S(1)}, f32[128,128]{1,0:T(8,128)S(1)}, u32[]{:S(2)}, u32[]{:S(2)}) collective-permute-start(f32[128,128]{1,0:T(8,128)S(1)} %log_add_fusion.4), channel_id=1, source_target_pairs={{0,16},{1,17},{2,18},{3,19},{4,20},{5,21},{6,22},{7,23},{8,24},{9,... | collective-permute-start | bytes 196616 | tf_op jit(solution)/shard_map/ppermute | solution.py:316
  56.6 5.2 %collective-permute-start.4 = (f32[128,128]{1,0:T(8,128)S(1)}, f32[128,128]{1,0:T(8,128)S(1)}, u32[]{:S(2)}, u32[]{:S(2)}) collective-permute-start(f32[128,128]{1,0:T(8,128)S(1)} %log_add_fusion.4), channel_id=1, source_target_pairs={{0,8},{1,9},{2,10},{3,11},{4,12},{5,13},{6,14},{7,15},{8,0},{9,1},... | collective-permute-start | bytes 196616 | tf_op jit(solution)/shard_map/ppermute | solution.py:316
  146.2 23.3 %collective-permute-start.7 = (f32[128,128]{1,0:T(8,128)S(1)}, f32[128,128]{1,0:T(8,128)S(1)}, u32[]{:S(2)}, u32[]{:S(2)}) collective-permute-start(f32[128,128]{1,0:T(8,128)S(1)} %src_next.1), channel_id=1, source_target_pairs={{0,1},{1,0},{2,3},{3,2},{4,5},{5,4},{6,7},{7,6},{8,9},{9,8},{10,11... | collective-permute-start | bytes 196616 | tf_op jit(solution)/shard_map/ppermute | solution.py:316
  169.6 7.1 %collective-permute-start.10 = (f32[128,128]{1,0:T(8,128)S(1)}, f32[128,128]{1,0:T(8,128)S(1)}, u32[]{:S(2)}, u32[]{:S(2)}) collective-permute-start(f32[128,128]{1,0:T(8,128)S(1)} %log_add_fusion.2), channel_id=1, source_target_pairs={{0,6},{1,7},{2,4},{3,5},{4,2},{5,3},{6,0},{7,1},{8,14},{9,15},{10,... | collective-permute-start | bytes 196616 | tf_op jit(solution)/shard_map/ppermute | solution.py:316
  169.7 7.0 %collective-permute-start.9 = (f32[128,128]{1,0:T(8,128)S(1)}, f32[128,128]{1,0:T(8,128)S(1)}, u32[]{:S(2)}, u32[]{:S(2)}) collective-permute-start(f32[128,128]{1,0:T(8,128)S(1)} %log_add_fusion.2), channel_id=1, source_target_pairs={{0,4},{1,5},{2,6},{3,7},{4,0},{5,1},{6,2},{7,3},{8,12},{9,13},{10,... | collective-permute-start | bytes 196616 | tf_op jit(solution)/shard_map/ppermute | solution.py:316
  169.8 7.4 %collective-permute-start.8 = (f32[128,128]{1,0:T(8,128)S(1)}, f32[128,128]{1,0:T(8,128)S(1)}, u32[]{:S(2)}, u32[]{:S(2)}) collective-permute-start(f32[128,128]{1,0:T(8,128)S(1)} %log_add_fusion.2), channel_id=1, source_target_pairs={{0,2},{1,3},{2,0},{3,1},{4,6},{5,7},{6,4},{7,5},{8,10},{9,11},{10,... | collective-permute-start | bytes 196616 | tf_op jit(solution)/shard_map/ppermute | solution.py:316
  177.3 4.9 %collective-permute-start.13 = (f32[128,128]{1,0:T(8,128)S(1)}, f32[128,128]{1,0:T(8,128)S(1)}, u32[]{:S(2)}, u32[]{:S(2)}) collective-permute-start(f32[128,128]{1,0:T(8,128)S(1)} %log_add_fusion.1), channel_id=1, source_target_pairs={{0,24},{1,25},{2,26},{3,27},{4,28},{5,29},{6,30},{7,31},{8,16},{9,... | collective-permute-start | bytes 196616 | tf_op jit(solution)/shard_map/ppermute | solution.py:316
  177.4 5.9 %collective-permute-start.12 = (f32[128,128]{1,0:T(8,128)S(1)}, f32[128,128]{1,0:T(8,128)S(1)}, u32[]{:S(2)}, u32[]{:S(2)}) collective-permute-start(f32[128,128]{1,0:T(8,128)S(1)} %log_add_fusion.1), channel_id=1, source_target_pairs={{0,16},{1,17},{2,18},{3,19},{4,20},{5,21},{6,22},{7,23},{8,24},{9,... | collective-permute-start | bytes 196616 | tf_op jit(solution)/shard_map/ppermute | solution.py:316
  177.5 6.9 %collective-permute-start.11 = (f32[128,128]{1,0:T(8,128)S(1)}, f32[128,128]{1,0:T(8,128)S(1)}, u32[]{:S(2)}, u32[]{:S(2)}) collective-permute-start(f32[128,128]{1,0:T(8,128)S(1)} %log_add_fusion.1), channel_id=1, source_target_pairs={{0,8},{1,9},{2,10},{3,11},{4,12},{5,13},{6,14},{7,15},{8,0},{9,1},... | collective-permute-start | bytes 196616 | tf_op jit(solution)/shard_map/ppermute | solution.py:316

commit v2 on v1

--- a/solution.py
+++ b/solution.py
@@ -11,8 +11,13 @@
 SWEEPS = 2
 ENTROPY = 0.5
 LOWEST = -1e30
+CHUNKS = 4
 GROUP = 8
-VMEM_LIMIT = 40 << 20
+HELD = 40
+HELD_GROUP = 4
+HELD_ROWS = 64
+VMEM_LIMIT = 7 << 20
+MERGE_LIMIT = 1 << 20
 
 
 def list_pairs(pattern_ref, list_ref):
@@ -39,11 +44,12 @@
 
 
 def factors(potential, reach):
-    shift = jnp.max(potential)
-    extent = shift - jnp.min(potential)
-    safe = jnp.logical_and(reach <= 70.0, reach + extent <= 80.0)
+    shift = jnp.max(potential, keepdims=True)
+    extent = shift - jnp.min(potential, keepdims=True)
+    fits = jnp.logical_and(reach <= 70.0, reach + extent <= 80.0)
     below = potential - shift
-    return jnp.where(safe, jnp.exp(below), below), shift, safe
+    safe = jnp.max(jnp.where(fits, 1.0, 0.0)) > 0.5
+    return jnp.where(fits, jnp.exp(below), below), shift, safe
 
 
 def log_or_lowest(total, top):
@@ -51,20 +57,20 @@
     return jnp.where(some, jnp.log(jnp.where(some, total, 1.0)) + top, LOWEST)
 
 
-def run_pairs(list_ref, visit):
-    count = list_ref[list_ref.shape[0] - 1]
-
+def run_pairs(list_ref, first, last, group, visit):
     def turn(width, base):
         def body(step, carry):
             for at in range(width):
-                visit(list_ref[base + step * width + at])
+                index = base + step * width + at
+                visit(index, list_ref[index])
             return carry
 
         return body
 
-    full = lax.div(count, GROUP)
-    lax.fori_loop(0, full, turn(GROUP, 0), 0)
-    lax.fori_loop(0, lax.div(count - full * GROUP + 1, 2), turn(2, full * GROUP), 0)
+    full = lax.div(last - first, group)
+    middle = first + full * group
+    lax.fori_loop(0, full, turn(group, first), 0)
+    lax.fori_loop(0, lax.div(last - middle + 1, 2), turn(2, middle), 0)
 
 
 def run_pairs_singly(list_ref, visit):
@@ -72,7 +78,15 @@
         visit(list_ref[step])
         return carry
 
-    lax.fori_loop(0, list_ref[list_ref.shape[0] - 1], body, 0)
+    lax.fori_loop(0, count_of(list_ref), body, 0)
+
+
+def count_of(list_ref):
+    return list_ref[list_ref.shape[0] - 2]
+
+
+def held_of(list_ref):
+    return list_ref[list_ref.shape[0] - 1]
 
 
 def place(pair, rows, cols):
@@ -102,24 +116,46 @@
         spread_ref[row * LANES : (row + 1) * LANES, :] = down
 
 
-def src_sums(potential, reach, list_ref, tall_ref, src_ref, spread_ref, sum_ref, top_ref, out_ref):
+def src_sums(
+    potential, reach, fill, list_ref, held_ref, tall_ref, src_ref, spread_ref, sum_ref, top_ref, out_ref
+):
     rows, cols = src_ref.shape[1] // BLOCK, tall_ref.shape[0] // BLOCK
     weights, shift, safe = factors(potential, reach)
     spread_down(weights, spread_ref)
     sum_ref[...] = jnp.zeros_like(sum_ref)
+    count = count_of(list_ref)
+    if fill:
+        list_ref[list_ref.shape[0] - 1] = jnp.where(safe, jnp.minimum(count, HELD), 0)
 
     @pl.when(safe)
     def _():
-        def visit(pair):
+        def visit(index, pair):
             src_block, tgt_block = place(pair, rows, cols)
             tile = jnp.exp(tile_of(tall_ref, src_ref, src_block, tgt_block))
+            if fill:
+                held_ref[jnp.minimum(index, HELD)] = tile
             down = spread_ref[pl.ds(pl.multiple_of(tgt_block * BLOCK, BLOCK), BLOCK), :]
             sums = [
                 (lane_part(tile, part) * down).reshape(-1, 8, LANES).sum(0) for part in range(PARTS)
             ]
             sum_ref[lax.div(pair, cols)] += jnp.concatenate(sums, axis=1)
 
-        run_pairs(list_ref, visit)
+        def visit_held(index, pair):
+            slot, base = jnp.minimum(index, HELD), lax.rem(pair, cols) * BLOCK
+            sums = [jnp.zeros((8, LANES), jnp.float32)] * PARTS
+            for start in range(0, BLOCK, HELD_ROWS):
+                down = spread_ref[pl.ds(pl.multiple_of(base + start, HELD_ROWS), HELD_ROWS), :]
+                for part in range(PARTS):
+                    lanes = slice(part * LANES, (part + 1) * LANES)
+                    tile = held_ref[slot, start : start + HELD_ROWS, lanes] * down
+                    sums[part] = sums[part] + tile.reshape(-1, 8, LANES).sum(0)
+            sum_ref[lax.div(pair, cols)] += jnp.concatenate(sums, axis=1)
+
+        held = 0
+        if not fill:
+            held = held_of(list_ref)
+            run_pairs(list_ref, 0, held, HELD_GROUP, visit_held)
+        run_pairs(list_ref, held, count, GROUP, visit)
         store_blocks(out_ref, log_or_lowest(sum_ref[0:rows].sum(1), shift))
 
     @pl.when(jnp.logical_not(safe))
@@ -150,7 +186,9 @@
         store_blocks(out_ref, log_or_lowest(total, top[:, 0] + shift))
 
 
-def tgt_sums(potential, reach, list_ref, tall_ref, src_ref, weight_ref, sum_ref, top_ref, out_ref):
+def tgt_sums(
+    potential, reach, list_ref, held_ref, tall_ref, src_ref, weight_ref, sum_ref, top_ref, out_ref
+):
     rows, cols = src_ref.shape[1] // BLOCK, tall_ref.shape[0] // BLOCK
     weights, shift, safe = factors(potential, reach)
     weight_ref[...] = weights
@@ -164,13 +202,24 @@
 
     @pl.when(safe)
     def _():
-        def visit(pair):
+        def visit(index, pair):
             src_block, tgt_block = place(pair, rows, cols)
             at = jnp.where(pair < rows * cols, tgt_block, cols)
             tile = jnp.exp(tile_of(tall_ref, src_ref, src_block, tgt_block))
             sum_ref[at] += fold_lanes(tile * weight_ref[pl.ds(src_block, 1), :], jnp.add)
 
-        run_pairs(list_ref, visit)
+        def visit_held(index, pair):
+            src_block, tgt_block = place(pair, rows, cols)
+            at = jnp.where(pair < rows * cols, tgt_block, cols)
+            slot = jnp.minimum(index, HELD)
+            right = weight_ref[pl.ds(src_block, 1), :]
+            for start in range(0, BLOCK, HELD_ROWS):
+                tile = held_ref[slot, start : start + HELD_ROWS, :] * right
+                sum_ref[at, start : start + HELD_ROWS, :] += fold_lanes(tile, jnp.add)
+
+        held = held_of(list_ref)
+        run_pairs(list_ref, 0, held, HELD_GROUP, visit_held)
+        run_pairs(list_ref, held, count_of(list_ref), GROUP, visit)
         for block in range(cols):
             store(block, sum_ref[block].T.sum(0, keepdims=True), shift)
 
@@ -206,8 +255,8 @@
         out_ref[copy] = out_ref[0]
 
 
-def store_squares(cells_ref, out_ref):
-    for block in range(cells_ref.shape[1] // BLOCK):
+def store_squares(cells_ref, out_ref, first, count):
+    for block in range(first, first + count):
         cells = cells_ref[:, block * BLOCK : (block + 1) * BLOCK].astype(jnp.float32)
         squares = jnp.sum(cells * cells, axis=0, keepdims=True)
         for part in range(PARTS):
@@ -216,40 +265,49 @@
 
 
 def first_src_kernel(
-    pattern_hbm, src_hbm, tgt_hbm, pot_hbm,
-    out_ref, src_ref, src_sq_ref, tgt_sq_ref, reach_ref, tall_ref, list_ref,
+    pattern_hbm, src_hbm, tgt_hbm, pot_hbm, room_ref,
+    out_ref, src_ref, src_sq_ref, tgt_sq_ref, reach_ref, tall_ref, list_ref, held_ref,
     pattern_ref, tgt_ref, pot_ref, sems, spread_ref, sum_ref, top_ref,
 ):
-    pattern_copy, tgt_copy, pot_copy, src_copy = copies = [
+    tgt_copy, pattern_copy, pot_copy = copies = [
         pltpu.make_async_copy(source, target, sems.at[at])
         for at, (source, target) in enumerate(
-            [(pattern_hbm, pattern_ref), (tgt_hbm, tgt_ref), (pot_hbm, pot_ref), (src_hbm, src_ref)]
+            [(tgt_hbm, tgt_ref), (pattern_hbm, pattern_ref), (pot_hbm, pot_ref)]
         )
     ]
-    for copy in copies:
+    width = src_ref.shape[1] // CHUNKS
+    src_copies = []
+    for chunk in range(CHUNKS):
+        lanes = pl.ds(chunk * width, width)
+        src_copies.append(
+            pltpu.make_async_copy(src_hbm.at[:, lanes], src_ref.at[:, lanes], sems.at[3 + chunk])
+        )
+    for copy in copies + src_copies:
         copy.start()
-    pattern_copy.wait()
-    list_pairs(pattern_ref, list_ref)
     tgt_copy.wait()
     for block in range(tgt_ref.shape[1] // BLOCK):
         cells = tgt_ref[:, block * BLOCK : (block + 1) * BLOCK].astype(jnp.float32) * 4.0
         tall_ref[block * BLOCK : (block + 1) * BLOCK, :] = cells.T.astype(jnp.bfloat16)
-    store_squares(tgt_ref, tgt_sq_ref)
+    store_squares(tgt_ref, tgt_sq_ref, 0, tgt_ref.shape[1] // BLOCK)
+    pattern_copy.wait()
+    list_pairs(pattern_ref, list_ref)
     pot_copy.wait()
-    src_copy.wait()
-    store_squares(src_ref, src_sq_ref)
+    for chunk in range(CHUNKS):
+        src_copies[chunk].wait()
+        store_squares(src_ref, src_sq_ref, chunk * width // BLOCK, width // BLOCK)
     reach = 4.0 * jnp.sqrt(jnp.max(src_sq_ref[...], keepdims=True)) * jnp.sqrt(
         jnp.max(tgt_sq_ref[...], keepdims=True)
     )
     reach_ref[...] = jnp.broadcast_to(reach, reach_ref.shape)
     potential = 2.0 * (pot_ref[...] - tgt_sq_ref[...])
     src_sums(
-        potential, jnp.max(reach), list_ref, tall_ref, src_ref, spread_ref, sum_ref, top_ref, out_ref
+        potential, reach, True, list_ref, held_ref, tall_ref, src_ref, spread_ref, sum_ref,
+        top_ref, out_ref,
     )
 
 
 def src_kernel(
-    list_ref, src_ref, tall_ref, gathered_ref, mass_ref, reach_ref,
+    list_ref, held_ref, src_ref, tall_ref, gathered_ref, mass_ref, reach_ref,
     out_ref,
     spread_ref, sum_ref, top_ref,
 ):
@@ -257,25 +315,25 @@
     top = gathered.max(0)
     potential = mass_ref[...] - (top + jnp.log(jnp.exp(gathered - top[None]).sum(0)))
     src_sums(
-        potential, jnp.max(reach_ref[...]), list_ref, tall_ref, src_ref, spread_ref, sum_ref, top_ref,
-        out_ref,
+        potential, reach_ref[0:1, 0:1], False, list_ref, held_ref, tall_ref, src_ref, spread_ref,
+        sum_ref, top_ref, out_ref,
     )
 
 
 def tgt_kernel(
-    list_ref, src_ref, tall_ref, logs_ref, mass_ref, reach_ref,
+    list_ref, held_ref, src_ref, tall_ref, logs_ref, mass_ref, reach_ref,
     out_ref,
     weight_ref, sum_ref, top_ref,
 ):
     potential = blocks_of(mass_ref) - blocks_of(logs_ref)
     tgt_sums(
-        potential, jnp.max(reach_ref[...]), list_ref, tall_ref, src_ref, weight_ref, sum_ref, top_ref,
-        out_ref,
+        potential, reach_ref[0:1, 0:1], list_ref, held_ref, tall_ref, src_ref, weight_ref, sum_ref,
+        top_ref, out_ref,
     )
 
 
 def last_tgt_kernel(
-    list_ref, src_ref, tall_ref, logs_ref, mass_ref, reach_ref, src_sq_ref,
+    list_ref, held_ref, src_ref, tall_ref, logs_ref, mass_ref, reach_ref, src_sq_ref,
     out_ref, src_pot_hbm,
     weight_ref, sum_ref, top_ref, src_pot_ref, sem,
 ):
@@ -283,20 +341,22 @@
     copy = pltpu.make_async_copy(src_pot_ref, src_pot_hbm, sem)
     copy.start()
     tgt_kernel(
-        list_ref, src_ref, tall_ref, logs_ref, mass_ref, reach_ref, out_ref, weight_ref, sum_ref, top_ref
+        list_ref, held_ref, src_ref, tall_ref, logs_ref, mass_ref, reach_ref, out_ref, weight_ref,
+        sum_ref, top_ref,
     )
     copy.wait()
 
 
-def call(kernel, args, in_spaces, outs, out_spaces, scratch, name):
+def call(kernel, args, in_spaces, outs, out_spaces, scratch, name, limit=VMEM_LIMIT, aliases={}):
     return pl.pallas_call(
         kernel,
         out_shape=outs,
         in_specs=[pl.BlockSpec(memory_space=space) for space in in_spaces],
         out_specs=[pl.BlockSpec(memory_space=space) for space in out_spaces],
         scratch_shapes=scratch,
-        compiler_params=pltpu.CompilerParams(vmem_limit_bytes=VMEM_LIMIT),
+        compiler_params=pltpu.CompilerParams(vmem_limit_bytes=limit),
         name=name,
+        input_output_aliases=aliases,
     )(*args)
 
 
@@ -304,9 +364,17 @@
     return jax.ShapeDtypeStruct(shape, jnp.float32)
 
 
-def combine(one, other):
-    top = jnp.maximum(one, other)
-    return top + jnp.log(1.0 + jnp.exp(-jnp.abs(one - other)))
+def merge_two_kernel(one_ref, other_ref, out_ref):
+    one, other = one_ref[...], other_ref[...]
+    out_ref[...] = jnp.maximum(one, other) + jnp.log(1.0 + jnp.exp(-jnp.abs(one - other)))
+
+
+def merge_kernel(own_ref, one_ref, two_ref, three_ref, out_ref):
+    own, one, two, three = own_ref[...], one_ref[...], two_ref[...], three_ref[...]
+    top = jnp.maximum(jnp.maximum(own, one), jnp.maximum(two, three))
+    near = jnp.exp(own - top) + jnp.exp(one - top)
+    far = jnp.exp(two - top) + jnp.exp(three - top)
+    out_ref[...] = top + jnp.log(near + far)
 
 
 def over_tgt(logs):
@@ -315,13 +383,16 @@
     def from_peer(values, mask):
         return lax.ppermute(values, "tgt", [(at, at ^ mask) for at in range(size)])
 
-    logs = combine(logs, from_peer(logs, 1))
+    (logs,) = call(
+        merge_two_kernel, [logs, from_peer(logs, 1)], [pltpu.VMEM] * 2, [floats(*logs.shape)],
+        [pltpu.VMEM], [], "merge_two", MERGE_LIMIT,
+    )
     for stage in (2, 8):
-        one, two, three = [from_peer(logs, stage * mask) for mask in (1, 2, 3)]
-        top = jnp.maximum(jnp.maximum(logs, one), jnp.maximum(two, three))
-        near = jnp.exp(logs - top) + jnp.exp(one - top)
-        far = jnp.exp(two - top) + jnp.exp(three - top)
-        logs = top + jnp.log(near + far)
+        peers = [from_peer(logs, stage * mask) for mask in (1, 2, 3)]
+        (logs,) = call(
+            merge_kernel, [logs] + peers, [pltpu.VMEM] * 4, [floats(*logs.shape)], [pltpu.VMEM], [],
+            "merge", MERGE_LIMIT,
+        )
     return logs
 
 
@@ -346,42 +417,49 @@
         vmem((cols + 1, BLOCK, LANES), jnp.float32),
         vmem((cols + 1, BLOCK, LANES), jnp.float32),
     ]
-    logs, src_held, src_sq, tgt_sq, reach, tall, pairs = call(
+    (room,) = call(
+        lambda room_ref: None, [], [], [vmem((HELD + 1, BLOCK, BLOCK), jnp.float32)], [vmem], [], "room",
+        MERGE_LIMIT,
+    )
+    logs, src_kept, src_sq, tgt_sq, reach, tall, pairs, held = call(
         first_src_kernel,
         [
             pltpu.with_memory_space_constraint(array, hbm)
             for array in (pattern.T, src_cells, tgt_cells, init_potential.reshape(tgt_shape))
-        ],
-        [hbm] * 4,
+        ]
+        + [pltpu.with_memory_space_constraint(room, vmem)],
+        [hbm] * 4 + [vmem],
         [
             floats(*src_shape), jax.ShapeDtypeStruct(src_cells.shape, src_cells.dtype),
             floats(*src_shape), floats(*tgt_shape), floats(8, LANES),
             jax.ShapeDtypeStruct((tgt_count, depth), jnp.bfloat16),
-            jax.ShapeDtypeStruct((rows * cols + GROUP + 1,), jnp.int32),
+            jax.ShapeDtypeStruct((rows * cols + GROUP + 2,), jnp.int32),
+            vmem((HELD + 1, BLOCK, BLOCK), jnp.float32),
         ],
-        [vmem] * 6 + [smem],
+        [vmem] * 6 + [smem, vmem],
         [
             smem((cols, rows), jnp.int32), vmem(tgt_cells.shape, tgt_cells.dtype),
-            vmem(tgt_shape, jnp.float32), pltpu.SemaphoreType.DMA((4,)),
+            vmem(tgt_shape, jnp.float32), pltpu.SemaphoreType.DMA((3 + CHUNKS,)),
         ] + src_scratch,
-        "src_first",
-    )
+        "src_first", aliases={4: 7},
+    )
+    held = pltpu.with_memory_space_constraint(held, vmem)
     for sweep in range(SWEEPS):
         if sweep:
             (logs,) = call(
-                src_kernel, [pairs, src_held, tall, gathered, tgt_mass, reach], [smem] + [vmem] * 5,
+                src_kernel, [pairs, held, src_kept, tall, gathered, tgt_mass, reach], [smem] + [vmem] * 6,
                 [floats(*src_shape)], [vmem], src_scratch, "src_next",
             )
-        src_logs = over_tgt(logs)
-        args = [pairs, src_held, tall, src_logs, src_mass, reach]
+        logs = over_tgt(logs)
+        args = [pairs, held, src_kept, tall, logs, src_mass, reach]
         if sweep < SWEEPS - 1:
             (logs,) = call(
-                tgt_kernel, args, [smem] + [vmem] * 5, [floats(copies, *tgt_shape)], [vmem],
+                tgt_kernel, args, [smem] + [vmem] * 6, [floats(copies, *tgt_shape)], [vmem],
                 tgt_scratch, "tgt",
             )
         else:
             logs, src_pot = call(
-                last_tgt_kernel, args + [src_sq], [smem] + [vmem] * 6,
+                last_tgt_kernel, args + [src_sq], [smem] + [vmem] * 7,
                 [floats(copies, *tgt_shape), floats(*src_shape)], [vmem, hbm],
                 tgt_scratch + [vmem(src_shape, jnp.float32), pltpu.SemaphoreType.DMA], "tgt_last",
             )

time: 246 us -> 247 us (level)
  the two profiles are of different devices: /device:TPU:8 before, /device:TPU:14 now
where the time goes in v2:
time: 247 us; the launch traced here: 248 us
  Pallas kernels  111 us (45%)
  blocking collectives  62.4 us (25%)
  starting transfers between devices  55.9 us (23%)
  waiting for transfers between devices  16.5 us (7%)
    pallas_call x11, Pallas kernels, call(): pl.pallas_call(kernel, out_shape=outs, in_specs=[pl.BlockSpec(memory_spac...  111 us
    all_to_all x2, blocking collectives, local(): gathered = lax.all_to_all(logs, 'src', 0, 0)  62.4 us
    ppermute x14, starting transfers between devices, from_peer(): return lax.ppermute(values, 'tgt', [(at, at ^ mask) for at in range(size)])  55.9 us
    ppermute x14, waiting for transfers between devices, from_peer(): return lax.ppermute(values, 'tgt', [(at, at ^ mask) for at in range(size)])  16.5 us
  transfers between devices with their start and end apart: 14, of which 11 were waited for; matrix products, arithmetic and copies ran while one was open for 0% of the time, Pallas kernels for 0%

profile of v2, /device:TPU:14, one launch (start us, length us, event | category | flops | bytes accessed | tf_op | source)
XLA Modules:
  0.0 247.7 jit_solution(11276761054587765932)
XLA Ops:
  0.7 30.1 %src_first.1 = (f32[128,128]{1,0:T(8,128)S(1)}, bf16[64,16384]{1,0:T(8,128)(2,1)S(1)}, f32[128,128]{1,0:T(8,128)S(1)}, f32[32,128]{1,0:T(8,128)S(1)}, f32[8,128]...) custom-call(s32[8,32]{1,0:T(8,128)} %bitcast.12, ...), custom_call_target="tpu_custom_call", output_to_operand_aliasing={{7}: (4, {})} | custom-call | tf_op jit(solution)/shard_map/src_first/pallas_call | solution.py:351
  30.8 6.3 %collective-permute-start = (f32[128,128]{1,0:T(8,128)S(1)}, f32[128,128]{1,0:T(8,128)S(1)}, u32[]{:S(2)}, u32[]{:S(2)}) collective-permute-start(f32[128,128]{1,0:T(8,128)S(1)} %get-tuple-element.16.one_ref), channel_id=1, source_target_pairs={{0,1},{1,0},{2,3},{3,2},{4,5},{5,4},{6,7},{7,6},{8,9},{9,8},{10,11... | collective-permute-start | bytes 196616 | tf_op jit(solution)/shard_map/ppermute | solution.py:384
  37.1 0.9 collective-permute-done.other_ref
  38.0 0.1 collective-permute-start.3
  38.1 12.4 %collective-permute-start.2 = (f32[128,128]{1,0:T(8,128)S(1)}, f32[128,128]{1,0:T(8,128)S(1)}, u32[]{:S(2)}, u32[]{:S(2)}) collective-permute-start(f32[128,128]{1,0:T(8,128)S(1)} %merge_two.2.own_ref), channel_id=1, source_target_pairs={{0,4},{1,5},{2,6},{3,7},{4,0},{5,1},{6,2},{7,3},{8,12},{9,13},{10,... | collective-permute-start | bytes 196616 | tf_op jit(solution)/shard_map/ppermute | solution.py:384
  50.5 2.2 collective-permute-done.2.two_ref
  52.7 2.0 collective-permute-done.1.one_ref
  54.8 0.1 merge.4.own_ref
  54.8 0.1 collective-permute-start.6
  54.9 1.7 collective-permute-start.5
  56.7 2.3 collective-permute-start.4
  59.0 0.2 collective-permute-done.6.three_ref
  59.2 1.6 collective-permute-done.5.two_ref
  60.8 1.2 collective-permute-done.4.one_ref
  62.0 0.1 merge.5.logs_ref
  62.0 26.6 %tgt.1 = f32[8,32,128]{2,1,0:T(8,128)S(1)} custom-call(s32[266]{0:T(512)S(1)} %get-tuple-element.12.list_ref, f32[41,512,512]{2,1,0:T(8,128)S(1)} %get-tuple-element.13.held_ref, bf16[64,16384]{1,0:T(8,128)(2,1)S(1)} %get-tuple-element.14.src_ref, bf16[4096,64]{1,0:T(8,128)(2,1)S(1)} %get-tuple-element.15.tall_ref, f32[128,128]{1,0:T(8,128)S(1)} %merge.5.logs_ref, ...), custom_call_target="tpu_custom_call" | custom-call | tf_op jit(solution)/shard_map/tgt/pallas_call | solution.py:351
  88.7 33.7 %all_to_all.10.gathered_ref = f32[8,32,128]{2,1,0:T(8,128)S(1)} all-to-all(f32[8,32,128]{2,1,0:T(8,128)S(1)} %tgt.1), channel_id=1, replica_groups=mesh['src'=8,'tgt'=32] {'src'}, dimensions={0} | all-to-all | bytes 262144 | tf_op jit(solution)/shard_map/all_to_all | solution.py:466
  122.3 28.0 %src_next.1.one_ref = f32[128,128]{1,0:T(8,128)S(1)} custom-call(s32[266]{0:T(512)S(1)} %get-tuple-element.12.list_ref, f32[41,512,512]{2,1,0:T(8,128)S(1)} %get-tuple-element.13.held_ref, bf16[64,16384]{1,0:T(8,128)(2,1)S(1)} %get-tuple-element.14.src_ref, bf16[4096,64]{1,0:T(8,128)(2,1)S(1)} %get-tuple-element.15.tall_ref, ...), custom_call_target="tpu_custom_call" | custom-call | tf_op jit(solution)/shard_map/src_next/pallas_call | solution.py:351
  150.3 4.7 %collective-permute-start.7 = (f32[128,128]{1,0:T(8,128)S(1)}, f32[128,128]{1,0:T(8,128)S(1)}, u32[]{:S(2)}, u32[]{:S(2)}) collective-permute-start(f32[128,128]{1,0:T(8,128)S(1)} %src_next.1.one_ref), channel_id=1, source_target_pairs={{0,1},{1,0},{2,3},{3,2},{4,5},{5,4},{6,7},{7,6},{8,9},{9,8},{10,11... | collective-permute-start | bytes 196616 | tf_op jit(solution)/shard_map/ppermute | solution.py:384
  155.0 0.9 collective-permute-done.7.other_ref
  155.9 0.1 collective-permute-start.10
  156.0 6.8 %collective-permute-start.9 = (f32[128,128]{1,0:T(8,128)S(1)}, f32[128,128]{1,0:T(8,128)S(1)}, u32[]{:S(2)}, u32[]{:S(2)}) collective-permute-start(f32[128,128]{1,0:T(8,128)S(1)} %merge_two.3.own_ref), channel_id=1, source_target_pairs={{0,4},{1,5},{2,6},{3,7},{4,0},{5,1},{6,2},{7,3},{8,12},{9,13},{10,... | collective-permute-start | bytes 196616 | tf_op jit(solution)/shard_map/ppermute | solution.py:384
  162.8 2.2 collective-permute-done.9.two_ref
  165.0 2.0 collective-permute-done.8.one_ref
  167.1 0.1 collective-permute-start.13
  167.2 20.2 %collective-permute-start.12 = (f32[128,128]{1,0:T(8,128)S(1)}, f32[128,128]{1,0:T(8,128)S(1)}, u32[]{:S(2)}, u32[]{:S(2)}) collective-permute-start(f32[128,128]{1,0:T(8,128)S(1)} %merge.6.own_ref), channel_id=1, source_target_pairs={{0,16},{1,17},{2,18},{3,19},{4,20},{5,21},{6,22},{7,23},{8,24},{9,... | collective-permute-start | bytes 196616 | tf_op jit(solution)/shard_map/ppermute | solution.py:384
  187.5 1.1 collective-permute-start.11
  188.5 1.2 collective-permute-done.12.two_ref
  189.7 2.0 collective-permute-done.11.one_ref
  191.8 26.5 %tgt_last.1 = (f32[8,32,128]{2,1,0:T(8,128)S(1)}, f32[128,128]{1,0:T(8,128)}) custom-call(s32[266]{0:T(512)S(1)} %get-tuple-element.12.list_ref, f32[41,512,512]{2,1,0:T(8,128)S(1)} %get-tuple-element.13.held_ref, bf16[64,16384]{1,0:T(8,128)(2,1)S(1)} %get-tuple-element.14.src_ref, bf16[4096,64]{1,0:T(8,128)(2,1)S(1)} %get-tuple-element.15.tall_ref, ...), custom_call_target="tpu_custom_call" | custom-call | tf_op jit(solution)/shard_map/tgt_last/pallas_call | solution.py:351
  218.3 28.8 %all_to_all.11 = f32[8,32,128]{2,1,0:T(8,128)S(1)} all-to-all(f32[8,32,128]{2,1,0:T(8,128)S(1)} %get-tuple-element.21), channel_id=1, replica_groups=mesh['src'=8,'tgt'=32] {'src'}, dimensions={0} | all-to-all | bytes 262144 | tf_op jit(solution)/shard_map/all_to_all | solution.py:466
  247.1 0.6 add_bitcast_fusion
  (16 shorter events, 0.3 us)
Async XLA Ops:
  0.6 61.4 %copy-start = (f32[16384]{0:T(1024)S(1)}, f32[16384]{0:T(1024)}, u32[]{:S(2)}) copy-start(f32[16384]{0:T(1024)} %param.8) | copy-start | bytes 196612
  0.6 121.7 %copy-start.1 = (f32[4096]{0:T(1024)S(1)}, f32[4096]{0:T(1024)}, u32[]{:S(2)}) copy-start(f32[4096]{0:T(1024)} %param.9) | copy-start | bytes 49156
  30.8 7.2 %collective-permute-start = (f32[128,128]{1,0:T(8,128)S(1)}, f32[128,128]{1,0:T(8,128)S(1)}, u32[]{:S(2)}, u32[]{:S(2)}) collective-permute-start(f32[128,128]{1,0:T(8,128)S(1)} %get-tuple-element.16.one_ref), channel_id=1, source_target_pairs={{0,1},{1,0},{2,3},{3,2},{4,5},{5,4},{6,7},{7,6},{8,9},{9,8},{10,11... | collective-permute-start | bytes 196616 | tf_op jit(solution)/shard_map/ppermute | solution.py:384
  38.0 12.5 %collective-permute-start.3 = (f32[128,128]{1,0:T(8,128)S(1)}, f32[128,128]{1,0:T(8,128)S(1)}, u32[]{:S(2)}, u32[]{:S(2)}) collective-permute-start(f32[128,128]{1,0:T(8,128)S(1)} %merge_two.2.own_ref), channel_id=1, source_target_pairs={{0,6},{1,7},{2,4},{3,5},{4,2},{5,3},{6,0},{7,1},{8,14},{9,15},{10,... | collective-permute-start | bytes 196616 | tf_op jit(solution)/shard_map/ppermute | solution.py:384
  38.1 14.6 %collective-permute-start.2 = (f32[128,128]{1,0:T(8,128)S(1)}, f32[128,128]{1,0:T(8,128)S(1)}, u32[]{:S(2)}, u32[]{:S(2)}) collective-permute-start(f32[128,128]{1,0:T(8,128)S(1)} %merge_two.2.own_ref), channel_id=1, source_target_pairs={{0,4},{1,5},{2,6},{3,7},{4,0},{5,1},{6,2},{7,3},{8,12},{9,13},{10,... | collective-permute-start | bytes 196616 | tf_op jit(solution)/shard_map/ppermute | solution.py:384
  50.5 4.3 %collective-permute-start.1 = (f32[128,128]{1,0:T(8,128)S(1)}, f32[128,128]{1,0:T(8,128)S(1)}, u32[]{:S(2)}, u32[]{:S(2)}) collective-permute-start(f32[128,128]{1,0:T(8,128)S(1)} %merge_two.2.own_ref), channel_id=1, source_target_pairs={{0,2},{1,3},{2,0},{3,1},{4,6},{5,7},{6,4},{7,5},{8,10},{9,11},{10,... | collective-permute-start | bytes 196616 | tf_op jit(solution)/shard_map/ppermute | solution.py:384
  54.8 4.4 %collective-permute-start.6 = (f32[128,128]{1,0:T(8,128)S(1)}, f32[128,128]{1,0:T(8,128)S(1)}, u32[]{:S(2)}, u32[]{:S(2)}) collective-permute-start(f32[128,128]{1,0:T(8,128)S(1)} %merge.4.own_ref), channel_id=1, source_target_pairs={{0,24},{1,25},{2,26},{3,27},{4,28},{5,29},{6,30},{7,31},{8,16},{9,... | collective-permute-start | bytes 196616 | tf_op jit(solution)/shard_map/ppermute | solution.py:384
  54.9 5.9 %collective-permute-start.5 = (f32[128,128]{1,0:T(8,128)S(1)}, f32[128,128]{1,0:T(8,128)S(1)}, u32[]{:S(2)}, u32[]{:S(2)}) collective-permute-start(f32[128,128]{1,0:T(8,128)S(1)} %merge.4.own_ref), channel_id=1, source_target_pairs={{0,16},{1,17},{2,18},{3,19},{4,20},{5,21},{6,22},{7,23},{8,24},{9,... | collective-permute-start | bytes 196616 | tf_op jit(solution)/shard_map/ppermute | solution.py:384
  56.7 5.3 %collective-permute-start.4 = (f32[128,128]{1,0:T(8,128)S(1)}, f32[128,128]{1,0:T(8,128)S(1)}, u32[]{:S(2)}, u32[]{:S(2)}) collective-permute-start(f32[128,128]{1,0:T(8,128)S(1)} %merge.4.own_ref), channel_id=1, source_target_pairs={{0,8},{1,9},{2,10},{3,11},{4,12},{5,13},{6,14},{7,15},{8,0},{9,1},... | collective-permute-start | bytes 196616 | tf_op jit(solution)/shard_map/ppermute | solution.py:384
  150.3 5.6 %collective-permute-start.7 = (f32[128,128]{1,0:T(8,128)S(1)}, f32[128,128]{1,0:T(8,128)S(1)}, u32[]{:S(2)}, u32[]{:S(2)}) collective-permute-start(f32[128,128]{1,0:T(8,128)S(1)} %src_next.1.one_ref), channel_id=1, source_target_pairs={{0,1},{1,0},{2,3},{3,2},{4,5},{5,4},{6,7},{7,6},{8,9},{9,8},{10,11... | collective-permute-start | bytes 196616 | tf_op jit(solution)/shard_map/ppermute | solution.py:384
  155.9 6.9 %collective-permute-start.10 = (f32[128,128]{1,0:T(8,128)S(1)}, f32[128,128]{1,0:T(8,128)S(1)}, u32[]{:S(2)}, u32[]{:S(2)}) collective-permute-start(f32[128,128]{1,0:T(8,128)S(1)} %merge_two.3.own_ref), channel_id=1, source_target_pairs={{0,6},{1,7},{2,4},{3,5},{4,2},{5,3},{6,0},{7,1},{8,14},{9,15},{10,... | collective-permute-start | bytes 196616 | tf_op jit(solution)/shard_map/ppermute | solution.py:384
  156.0 9.0 %collective-permute-start.9 = (f32[128,128]{1,0:T(8,128)S(1)}, f32[128,128]{1,0:T(8,128)S(1)}, u32[]{:S(2)}, u32[]{:S(2)}) collective-permute-start(f32[128,128]{1,0:T(8,128)S(1)} %merge_two.3.own_ref), channel_id=1, source_target_pairs={{0,4},{1,5},{2,6},{3,7},{4,0},{5,1},{6,2},{7,3},{8,12},{9,13},{10,... | collective-permute-start | bytes 196616 | tf_op jit(solution)/shard_map/ppermute | solution.py:384
  162.8 4.3 %collective-permute-start.8 = (f32[128,128]{1,0:T(8,128)S(1)}, f32[128,128]{1,0:T(8,128)S(1)}, u32[]{:S(2)}, u32[]{:S(2)}) collective-permute-start(f32[128,128]{1,0:T(8,128)S(1)} %merge_two.3.own_ref), channel_id=1, source_target_pairs={{0,2},{1,3},{2,0},{3,1},{4,6},{5,7},{6,4},{7,5},{8,10},{9,11},{10,... | collective-permute-start | bytes 196616 | tf_op jit(solution)/shard_map/ppermute | solution.py:384
  167.1 21.4 %collective-permute-start.13 = (f32[128,128]{1,0:T(8,128)S(1)}, f32[128,128]{1,0:T(8,128)S(1)}, u32[]{:S(2)}, u32[]{:S(2)}) collective-permute-start(f32[128,128]{1,0:T(8,128)S(1)} %merge.6.own_ref), channel_id=1, source_target_pairs={{0,24},{1,25},{2,26},{3,27},{4,28},{5,29},{6,30},{7,31},{8,16},{9,... | collective-permute-start | bytes 196616 | tf_op jit(solution)/shard_map/ppermute | solution.py:384
  167.2 22.5 %collective-permute-start.12 = (f32[128,128]{1,0:T(8,128)S(1)}, f32[128,128]{1,0:T(8,128)S(1)}, u32[]{:S(2)}, u32[]{:S(2)}) collective-permute-start(f32[128,128]{1,0:T(8,128)S(1)} %merge.6.own_ref), channel_id=1, source_target_pairs={{0,16},{1,17},{2,18},{3,19},{4,20},{5,21},{6,22},{7,23},{8,24},{9,... | collective-permute-start | bytes 196616 | tf_op jit(solution)/shard_map/ppermute | solution.py:384
  187.5 4.3 %collective-permute-start.11 = (f32[128,128]{1,0:T(8,128)S(1)}, f32[128,128]{1,0:T(8,128)S(1)}, u32[]{:S(2)}, u32[]{:S(2)}) collective-permute-start(f32[128,128]{1,0:T(8,128)S(1)} %merge.6.own_ref), channel_id=1, source_target_pairs={{0,8},{1,9},{2,10},{3,11},{4,12},{5,13},{6,14},{7,15},{8,0},{9,1},... | collective-permute-start | bytes 196616 | tf_op jit(solution)/shard_map/ppermute | solution.py:384

commit v3 on v2

--- a/solution.py
+++ b/solution.py
@@ -13,8 +13,8 @@
 LOWEST = -1e30
 CHUNKS = 4
 GROUP = 8
-HELD = 40
-HELD_GROUP = 4
+HELD = 42
+HELD_GROUP = 6
 HELD_ROWS = 64
 VMEM_LIMIT = 7 << 20
 MERGE_LIMIT = 1 << 20
@@ -285,16 +285,16 @@
     for copy in copies + src_copies:
         copy.start()
     tgt_copy.wait()
+    pattern_copy.wait()
+    list_pairs(pattern_ref, list_ref)
     for block in range(tgt_ref.shape[1] // BLOCK):
         cells = tgt_ref[:, block * BLOCK : (block + 1) * BLOCK].astype(jnp.float32) * 4.0
         tall_ref[block * BLOCK : (block + 1) * BLOCK, :] = cells.T.astype(jnp.bfloat16)
     store_squares(tgt_ref, tgt_sq_ref, 0, tgt_ref.shape[1] // BLOCK)
-    pattern_copy.wait()
-    list_pairs(pattern_ref, list_ref)
     pot_copy.wait()
-    for chunk in range(CHUNKS):
-        src_copies[chunk].wait()
-        store_squares(src_ref, src_sq_ref, chunk * width // BLOCK, width // BLOCK)
+    for copy in src_copies:
+        copy.wait()
+    store_squares(src_ref, src_sq_ref, 0, src_ref.shape[1] // BLOCK)
     reach = 4.0 * jnp.sqrt(jnp.max(src_sq_ref[...], keepdims=True)) * jnp.sqrt(
         jnp.max(tgt_sq_ref[...], keepdims=True)
     )

time: 247 us -> 260 us (1.053)
  the two profiles are of different devices: /device:TPU:14 before, /device:TPU:2 now
where the time goes in v3:
time: 260 us; the launch traced here: 258 us
  Pallas kernels  202 us (78%)
  blocking collectives  23.1 us (9%)
  starting transfers between devices  16.8 us (6%)
  waiting for transfers between devices  14.9 us (6%)
    pallas_call x11, Pallas kernels, call(): pl.pallas_call(kernel, out_shape=outs, in_specs=[pl.BlockSpec(memory_spac...  202 us
    all_to_all x2, blocking collectives, local(): gathered = lax.all_to_all(logs, 'src', 0, 0)  23.1 us
    ppermute x14, starting transfers between devices, from_peer(): return lax.ppermute(values, 'tgt', [(at, at ^ mask) for at in range(size)])  16.8 us
    ppermute x14, waiting for transfers between devices, from_peer(): return lax.ppermute(values, 'tgt', [(at, at ^ mask) for at in range(size)])  14.9 us
  transfers between devices with their start and end apart: 14, of which 12 were waited for; matrix products, arithmetic and copies ran while one was open for 0% of the time, Pallas kernels for 0%

profile of v3, /device:TPU:2, one launch (start us, length us, event | category | flops | bytes accessed | tf_op | source)
XLA Modules:
  0.0 258.5 jit_solution(490077155315598260)
XLA Ops:
  0.7 53.6 %src_first.1 = (f32[128,128]{1,0:T(8,128)S(1)}, bf16[64,16384]{1,0:T(8,128)(2,1)S(1)}, f32[128,128]{1,0:T(8,128)S(1)}, f32[32,128]{1,0:T(8,128)S(1)}, f32[8,128]...) custom-call(s32[8,32]{1,0:T(8,128)} %bitcast.12, ...), custom_call_target="tpu_custom_call", output_to_operand_aliasing={{7}: (4, {})} | custom-call | tf_op jit(solution)/shard_map/src_first/pallas_call | solution.py:351
  54.2 0.1 collective-permute-start
  54.3 1.2 collective-permute-done.other_ref
  55.6 0.1 collective-permute-start.3
  55.7 0.1 collective-permute-start.2
  55.8 4.0 %collective-permute-start.1 = (f32[128,128]{1,0:T(8,128)S(1)}, f32[128,128]{1,0:T(8,128)S(1)}, u32[]{:S(2)}, u32[]{:S(2)}) collective-permute-start(f32[128,128]{1,0:T(8,128)S(1)} %merge_two.2.own_ref), channel_id=1, source_target_pairs={{0,2},{1,3},{2,0},{3,1},{4,6},{5,7},{6,4},{7,5},{8,10},{9,11},{10,... | collective-permute-start | bytes 196616 | tf_op jit(solution)/shard_map/ppermute | solution.py:384
  59.8 0.2 collective-permute-done.3.three_ref
  60.0 2.2 collective-permute-done.2.two_ref
  62.2 0.9 collective-permute-done.1.one_ref
  63.1 0.1 collective-permute-start.6
  63.3 4.0 %collective-permute-start.4 = (f32[128,128]{1,0:T(8,128)S(1)}, f32[128,128]{1,0:T(8,128)S(1)}, u32[]{:S(2)}, u32[]{:S(2)}) collective-permute-start(f32[128,128]{1,0:T(8,128)S(1)} %merge.4.own_ref), channel_id=1, source_target_pairs={{0,8},{1,9},{2,10},{3,11},{4,12},{5,13},{6,14},{7,15},{8,0},{9,1},... | collective-permute-start | bytes 196616 | tf_op jit(solution)/shard_map/ppermute | solution.py:384
  67.3 2.1 collective-permute-done.6.three_ref
  69.4 0.9 collective-permute-done.4.one_ref
  70.3 48.4 %tgt.1 = f32[8,32,128]{2,1,0:T(8,128)S(1)} custom-call(s32[266]{0:T(512)S(1)} %get-tuple-element.12.list_ref, f32[43,512,512]{2,1,0:T(8,128)S(1)} %get-tuple-element.13.held_ref, bf16[64,16384]{1,0:T(8,128)(2,1)S(1)} %get-tuple-element.14.src_ref, bf16[4096,64]{1,0:T(8,128)(2,1)S(1)} %get-tuple-element.15.tall_ref, f32[128,128]{1,0:T(8,128)S(1)} %merge.5.logs_ref, ...), custom_call_target="tpu_custom_call" | custom-call | tf_op jit(solution)/shard_map/tgt/pallas_call | solution.py:351
  118.7 11.6 %all_to_all.10.gathered_ref = f32[8,32,128]{2,1,0:T(8,128)S(1)} all-to-all(f32[8,32,128]{2,1,0:T(8,128)S(1)} %tgt.1), channel_id=1, replica_groups=mesh['src'=8,'tgt'=32] {'src'}, dimensions={0} | all-to-all | bytes 262144 | tf_op jit(solution)/shard_map/all_to_all | solution.py:466
  130.3 51.5 %src_next.1.one_ref = f32[128,128]{1,0:T(8,128)S(1)} custom-call(s32[266]{0:T(512)S(1)} %get-tuple-element.12.list_ref, f32[43,512,512]{2,1,0:T(8,128)S(1)} %get-tuple-element.13.held_ref, bf16[64,16384]{1,0:T(8,128)(2,1)S(1)} %get-tuple-element.14.src_ref, bf16[4096,64]{1,0:T(8,128)(2,1)S(1)} %get-tuple-element.15.tall_ref, ...), custom_call_target="tpu_custom_call" | custom-call | tf_op jit(solution)/shard_map/src_next/pallas_call | solution.py:351
  181.9 0.1 collective-permute-start.7
  182.0 1.2 collective-permute-done.7.other_ref
  183.3 0.1 collective-permute-start.10
  183.4 0.1 collective-permute-start.9
  183.5 4.0 %collective-permute-start.8 = (f32[128,128]{1,0:T(8,128)S(1)}, f32[128,128]{1,0:T(8,128)S(1)}, u32[]{:S(2)}, u32[]{:S(2)}) collective-permute-start(f32[128,128]{1,0:T(8,128)S(1)} %merge_two.3.own_ref), channel_id=1, source_target_pairs={{0,2},{1,3},{2,0},{3,1},{4,6},{5,7},{6,4},{7,5},{8,10},{9,11},{10,... | collective-permute-start | bytes 196616 | tf_op jit(solution)/shard_map/ppermute | solution.py:384
  187.4 0.2 collective-permute-done.10.three_ref
  187.6 2.2 collective-permute-done.9.two_ref
  189.8 0.9 collective-permute-done.8.one_ref
  190.8 0.1 collective-permute-start.13
  190.9 0.1 collective-permute-start.12
  191.0 4.0 %collective-permute-start.11 = (f32[128,128]{1,0:T(8,128)S(1)}, f32[128,128]{1,0:T(8,128)S(1)}, u32[]{:S(2)}, u32[]{:S(2)}) collective-permute-start(f32[128,128]{1,0:T(8,128)S(1)} %merge.6.own_ref), channel_id=1, source_target_pairs={{0,8},{1,9},{2,10},{3,11},{4,12},{5,13},{6,14},{7,15},{8,0},{9,1},... | collective-permute-start | bytes 196616 | tf_op jit(solution)/shard_map/ppermute | solution.py:384
  194.9 2.1 collective-permute-done.13.three_ref
  197.0 0.9 collective-permute-done.11.one_ref
  197.9 48.4 %tgt_last.1 = (f32[8,32,128]{2,1,0:T(8,128)S(1)}, f32[128,128]{1,0:T(8,128)}) custom-call(s32[266]{0:T(512)S(1)} %get-tuple-element.12.list_ref, f32[43,512,512]{2,1,0:T(8,128)S(1)} %get-tuple-element.13.held_ref, bf16[64,16384]{1,0:T(8,128)(2,1)S(1)} %get-tuple-element.14.src_ref, bf16[4096,64]{1,0:T(8,128)(2,1)S(1)} %get-tuple-element.15.tall_ref, ...), custom_call_target="tpu_custom_call" | custom-call | tf_op jit(solution)/shard_map/tgt_last/pallas_call | solution.py:351
  246.4 11.5 %all_to_all.11 = f32[8,32,128]{2,1,0:T(8,128)S(1)} all-to-all(f32[8,32,128]{2,1,0:T(8,128)S(1)} %get-tuple-element.21), channel_id=1, replica_groups=mesh['src'=8,'tgt'=32] {'src'}, dimensions={0} | all-to-all | bytes 262144 | tf_op jit(solution)/shard_map/all_to_all | solution.py:466
  257.9 0.6 add_bitcast_fusion
  (16 shorter events, 0.5 us)
Async XLA Ops:
  0.6 69.7 %copy-start = (f32[16384]{0:T(1024)S(1)}, f32[16384]{0:T(1024)}, u32[]{:S(2)}) copy-start(f32[16384]{0:T(1024)} %param.8) | copy-start | bytes 196612
  0.6 129.7 %copy-start.1 = (f32[4096]{0:T(1024)S(1)}, f32[4096]{0:T(1024)}, u32[]{:S(2)}) copy-start(f32[4096]{0:T(1024)} %param.9) | copy-start | bytes 49156
  54.2 1.3 collective-permute-start
  55.6 4.4 %collective-permute-start.3 = (f32[128,128]{1,0:T(8,128)S(1)}, f32[128,128]{1,0:T(8,128)S(1)}, u32[]{:S(2)}, u32[]{:S(2)}) collective-permute-start(f32[128,128]{1,0:T(8,128)S(1)} %merge_two.2.own_ref), channel_id=1, source_target_pairs={{0,6},{1,7},{2,4},{3,5},{4,2},{5,3},{6,0},{7,1},{8,14},{9,15},{10,... | collective-permute-start | bytes 196616 | tf_op jit(solution)/shard_map/ppermute | solution.py:384
  55.7 6.4 %collective-permute-start.2 = (f32[128,128]{1,0:T(8,128)S(1)}, f32[128,128]{1,0:T(8,128)S(1)}, u32[]{:S(2)}, u32[]{:S(2)}) collective-permute-start(f32[128,128]{1,0:T(8,128)S(1)} %merge_two.2.own_ref), channel_id=1, source_target_pairs={{0,4},{1,5},{2,6},{3,7},{4,0},{5,1},{6,2},{7,3},{8,12},{9,13},{10,... | collective-permute-start | bytes 196616 | tf_op jit(solution)/shard_map/ppermute | solution.py:384
  55.8 7.2 %collective-permute-start.1 = (f32[128,128]{1,0:T(8,128)S(1)}, f32[128,128]{1,0:T(8,128)S(1)}, u32[]{:S(2)}, u32[]{:S(2)}) collective-permute-start(f32[128,128]{1,0:T(8,128)S(1)} %merge_two.2.own_ref), channel_id=1, source_target_pairs={{0,2},{1,3},{2,0},{3,1},{4,6},{5,7},{6,4},{7,5},{8,10},{9,11},{10,... | collective-permute-start | bytes 196616 | tf_op jit(solution)/shard_map/ppermute | solution.py:384
  63.1 6.3 %collective-permute-start.6 = (f32[128,128]{1,0:T(8,128)S(1)}, f32[128,128]{1,0:T(8,128)S(1)}, u32[]{:S(2)}, u32[]{:S(2)}) collective-permute-start(f32[128,128]{1,0:T(8,128)S(1)} %merge.4.own_ref), channel_id=1, source_target_pairs={{0,24},{1,25},{2,26},{3,27},{4,28},{5,29},{6,30},{7,31},{8,16},{9,... | collective-permute-start | bytes 196616 | tf_op jit(solution)/shard_map/ppermute | solution.py:384
  63.2 6.2 %collective-permute-start.5 = (f32[128,128]{1,0:T(8,128)S(1)}, f32[128,128]{1,0:T(8,128)S(1)}, u32[]{:S(2)}, u32[]{:S(2)}) collective-permute-start(f32[128,128]{1,0:T(8,128)S(1)} %merge.4.own_ref), channel_id=1, source_target_pairs={{0,16},{1,17},{2,18},{3,19},{4,20},{5,21},{6,22},{7,23},{8,24},{9,... | collective-permute-start | bytes 196616 | tf_op jit(solution)/shard_map/ppermute | solution.py:384
  63.3 6.9 %collective-permute-start.4 = (f32[128,128]{1,0:T(8,128)S(1)}, f32[128,128]{1,0:T(8,128)S(1)}, u32[]{:S(2)}, u32[]{:S(2)}) collective-permute-start(f32[128,128]{1,0:T(8,128)S(1)} %merge.4.own_ref), channel_id=1, source_target_pairs={{0,8},{1,9},{2,10},{3,11},{4,12},{5,13},{6,14},{7,15},{8,0},{9,1},... | collective-permute-start | bytes 196616 | tf_op jit(solution)/shard_map/ppermute | solution.py:384
  181.9 1.3 collective-permute-start.7
  183.3 4.4 %collective-permute-start.10 = (f32[128,128]{1,0:T(8,128)S(1)}, f32[128,128]{1,0:T(8,128)S(1)}, u32[]{:S(2)}, u32[]{:S(2)}) collective-permute-start(f32[128,128]{1,0:T(8,128)S(1)} %merge_two.3.own_ref), channel_id=1, source_target_pairs={{0,6},{1,7},{2,4},{3,5},{4,2},{5,3},{6,0},{7,1},{8,14},{9,15},{10,... | collective-permute-start | bytes 196616 | tf_op jit(solution)/shard_map/ppermute | solution.py:384
  183.4 6.4 %collective-permute-start.9 = (f32[128,128]{1,0:T(8,128)S(1)}, f32[128,128]{1,0:T(8,128)S(1)}, u32[]{:S(2)}, u32[]{:S(2)}) collective-permute-start(f32[128,128]{1,0:T(8,128)S(1)} %merge_two.3.own_ref), channel_id=1, source_target_pairs={{0,4},{1,5},{2,6},{3,7},{4,0},{5,1},{6,2},{7,3},{8,12},{9,13},{10,... | collective-permute-start | bytes 196616 | tf_op jit(solution)/shard_map/ppermute | solution.py:384
  183.5 7.2 %collective-permute-start.8 = (f32[128,128]{1,0:T(8,128)S(1)}, f32[128,128]{1,0:T(8,128)S(1)}, u32[]{:S(2)}, u32[]{:S(2)}) collective-permute-start(f32[128,128]{1,0:T(8,128)S(1)} %merge_two.3.own_ref), channel_id=1, source_target_pairs={{0,2},{1,3},{2,0},{3,1},{4,6},{5,7},{6,4},{7,5},{8,10},{9,11},{10,... | collective-permute-start | bytes 196616 | tf_op jit(solution)/shard_map/ppermute | solution.py:384
  190.8 6.3 %collective-permute-start.13 = (f32[128,128]{1,0:T(8,128)S(1)}, f32[128,128]{1,0:T(8,128)S(1)}, u32[]{:S(2)}, u32[]{:S(2)}) collective-permute-start(f32[128,128]{1,0:T(8,128)S(1)} %merge.6.own_ref), channel_id=1, source_target_pairs={{0,24},{1,25},{2,26},{3,27},{4,28},{5,29},{6,30},{7,31},{8,16},{9,... | collective-permute-start | bytes 196616 | tf_op jit(solution)/shard_map/ppermute | solution.py:384
  190.9 6.2 %collective-permute-start.12 = (f32[128,128]{1,0:T(8,128)S(1)}, f32[128,128]{1,0:T(8,128)S(1)}, u32[]{:S(2)}, u32[]{:S(2)}) collective-permute-start(f32[128,128]{1,0:T(8,128)S(1)} %merge.6.own_ref), channel_id=1, source_target_pairs={{0,16},{1,17},{2,18},{3,19},{4,20},{5,21},{6,22},{7,23},{8,24},{9,... | collective-permute-start | bytes 196616 | tf_op jit(solution)/shard_map/ppermute | solution.py:384
  191.0 6.9 %collective-permute-start.11 = (f32[128,128]{1,0:T(8,128)S(1)}, f32[128,128]{1,0:T(8,128)S(1)}, u32[]{:S(2)}, u32[]{:S(2)}) collective-permute-start(f32[128,128]{1,0:T(8,128)S(1)} %merge.6.own_ref), channel_id=1, source_target_pairs={{0,8},{1,9},{2,10},{3,11},{4,12},{5,13},{6,14},{7,15},{8,0},{9,1},... | collective-permute-start | bytes 196616 | tf_op jit(solution)/shard_map/ppermute | solution.py:384
